TPU v7x, 256 devices: a whole 4x4x8 slice. The times are simulated.
256 devices in a mesh: section: 2 (over x_lo), dp: 16 (over z, core), tensor: 8 (over y, x_hi).
Axes of the slice: x: 4 (x_hi: 2, x_lo: 2; x = x_hi * 2 + x_lo), y: 4, z: 8, core: 2. Of those that a mesh axis runs over, the one named last changes fastest.
Arguments:
- cache_keys: bfloat16 [2, 256, 512, 1024], P(None, ('section', 'dp'), None, 'tensor'), may hold values from -5 to 5
- cache_values: bfloat16 [2, 256, 512, 1024], P(None, ('section', 'dp'), None, 'tensor'), may hold values from -5 to 5
- span_ids: int32 [32, 8], P('dp'), may hold values from 0 to 255, as said below
- owner_slot: int32 [256], replicated, may hold values from 0 to 255, as said below
- recompute_rows: int32 [256, 76], replicated, may hold values from 0 to 511, as said below
- hidden: bfloat16 [2, 32, 8, 76, 8192], P('section', 'dp', None, None, 'tensor'), may hold values from -6 to 6
- w_key: bfloat16 [2, 8192, 1024], P('section', 'tensor'), may hold values from -0.0625 to 0.0625
- w_value: bfloat16 [2, 8192, 1024], P('section', 'tensor'), may hold values from -0.0625 to 0.0625
- queries: bfloat16 [2, 32, 256, 8192], P('section', 'dp', None, 'tensor')
- query_keys: bfloat16 [2, 32, 256, 1024], P('section', 'dp', None, 'tensor')
- query_values: bfloat16 [2, 32, 256, 1024], P('section', 'dp', None, 'tensor'), may hold values from -5 to 5
Outputs:
- attended: bfloat16 [2, 32, 256, 8192], P('section', 'dp', None, 'tensor')
Inputs may be any that keep to these rules, and one draw needn't show every extreme that they name: `owner_slot`: A permutation: each storage row holds one span; the owner of storage row s is the device s // 8 of section+dp. `span_ids`: the 16 spans named by the requests of one dp index lie on as many different owners. `recompute_rows`: each span's 76 rows are different.
All inputs are finite; a program needn't handle non-finite values.
Results may differ from a plain program's by a relative error of at most 0.02.
Values may be sent and summed in bfloat16 or wider, within the bound.
No kernel may reach another device: no remote copies, remote signals or barrier semaphores. Data moves between devices by JAX's collectives and lax.ppermute only.
A program may use at most 128 MiB of HBM per device.

v0:
```python
import jax
import jax.numpy as jnp
from jax import lax
from jax.sharding import PartitionSpec as P

HD = 128


def attend_block(query_rows, keys, values, start, context):
    count = query_rows.shape[0]
    heads_kv = keys.shape[1] // HD
    scale = 1.0 / jnp.sqrt(jnp.float32(HD))
    queried = query_rows.reshape(count, heads_kv, -1, HD)
    keyed = keys.reshape(-1, heads_kv, HD)
    valued = values.reshape(-1, heads_kv, HD)
    scores = (
        jnp.einsum("qkgd,nkd->kgqn", queried, keyed, preferred_element_type=jnp.float32) * scale
    )
    col = jnp.arange(keys.shape[0], dtype=jnp.int32)[None, :]
    row = start + jnp.arange(count, dtype=jnp.int32)[:, None]
    allowed = (col < context) | (col - context <= row)
    scores = jnp.where(allowed, scores, jnp.float32(-1e30))
    top = jnp.max(scores, axis=-1, keepdims=True)
    expo = jnp.exp(scores - top)
    probs = (expo / jnp.sum(expo, axis=-1, keepdims=True)).astype(jnp.bfloat16)
    out = jnp.einsum("kgqn,nkd->qkgd", probs, valued, preferred_element_type=jnp.float32)
    return out.reshape(count, -1).astype(jnp.bfloat16)


def on_device(
    cache_keys,
    cache_values,
    span_ids,
    owner_slot,
    recompute_rows,
    hidden,
    w_key,
    w_value,
    queries,
    query_keys,
    query_values,
):
    sections = lax.axis_size("section")
    groups = lax.axis_size("dp")
    parts = lax.axis_size("tensor")
    owners = sections * groups
    per_owner = cache_keys.shape[1]
    clen = cache_keys.shape[2]
    width = cache_keys.shape[3]
    req_dev, topk = span_ids.shape
    rrows = hidden.shape[3]
    every_list = lax.all_gather(span_ids, "dp", axis=0, tiled=True)
    myself = lax.axis_index("section") * groups + lax.axis_index("dp")
    every_slot = owner_slot[every_list].reshape(groups, req_dev * topk)
    mine = every_slot // per_owner == myself
    local_row = jnp.sum(jnp.where(mine, every_slot % per_owner, 0), axis=1)
    present = jnp.any(mine, axis=1)
    picked_k = jnp.take(cache_keys, local_row, axis=1)
    picked_v = jnp.take(cache_values, local_row, axis=1)
    outgoing = jnp.concatenate([picked_k, picked_v], axis=3)
    outgoing = jnp.where(present[None, :, None, None], outgoing, jnp.zeros_like(outgoing))
    own_slot = owner_slot[span_ids]
    picked_rows = recompute_rows[span_ids].reshape(req_dev * topk, rrows)
    base_rows = jnp.arange(req_dev * topk, dtype=jnp.int32)[:, None] * clen
    arrived = lax.all_to_all(
        outgoing.reshape(owners, clen, 2 * width),
        ("section", "dp"),
        split_axis=0,
        concat_axis=0,
        tiled=True,
    )
    fetched = arrived[own_slot // per_owner].reshape(-1, 2 * width)
    rows = hidden[0].reshape(-1, hidden.shape[-1])
    share = w_key.shape[2] // parts
    joined = jnp.concatenate(
        [w_key[0].reshape(-1, parts, share), w_value[0].reshape(-1, parts, share)], axis=2
    ).reshape(rows.shape[1], -1)
    summed = lax.psum_scatter(
        lax.dot_general(
            joined, rows, (((0,), (1,)), ((), ())), preferred_element_type=jnp.float32
        ).astype(jnp.bfloat16),
        "tensor",
        scatter_dimension=0,
        tiled=True,
    ).astype(jnp.float32)
    fresh = summed.T.astype(jnp.bfloat16)
    flat = (base_rows + picked_rows).reshape(-1)
    merged = fetched.at[flat].set(fresh).reshape(req_dev, topk * clen, 2 * width)
    context = topk * clen
    qlen = queries.shape[2]
    qblock = 128
    blocks = qlen // qblock
    starts = jnp.arange(blocks, dtype=jnp.int32) * qblock
    results = []
    for request in range(req_dev):
        keys = jnp.concatenate([merged[request, :, :width], query_keys[0, request]], axis=0)
        values = jnp.concatenate([merged[request, :, width:], query_values[0, request]], axis=0)
        query_blocks = queries[0, request].reshape(blocks, qblock, -1)

        def one_block(items):
            return attend_block(items[0], keys, values, items[1], context)

        results.append(lax.map(one_block, (query_blocks, starts)).reshape(qlen, -1))
    return jnp.stack(results)[None]


def solution(mesh):
    in_specs = (
        P(None, ("section", "dp"), None, "tensor"),
        P(None, ("section", "dp"), None, "tensor"),
        P("dp", None),
        P(),
        P(),
        P("section", "dp", None, None, "tensor"),
        P("section", "tensor", None),
        P("section", "tensor", None),
        P("section", "dp", None, "tensor"),
        P("section", "dp", None, "tensor"),
        P("section", "dp", None, "tensor"),
    )
    out_specs = P("section", "dp", None, "tensor")
    return jax.shard_map(
        on_device, mesh=mesh, in_specs=in_specs, out_specs=out_specs, check_vma=False
    )
```

profile of v0, /device:TPU:1, one launch (start us, length us, event | category | flops | bytes accessed | tf_op | source)
XLA Modules:
  0.0 405.1 jit_solution(16140500212715585430)
XLA Ops:
  6.5 21.7 %all-gather = s32[16,2,8]{2,1,0:T(2,128)S(1)} all-gather(s32[1,2,8]{2,1,0:T(2,128)} %bitcast.186), channel_id=1, replica_groups=mesh['section'=2,'dp'=16,'tensor'=8] {'dp'}, dimensions={0}, use_global_device_ids=true | all-gather | bytes 1088 | tf_op jit(solution)/shard_map/all_gather | solution.py:52
  30.9 3.0 gather_fusion.4
  33.9 4.6 %gather_fusion.5 = bf16[16,2,512,128]{3,2,1,0:T(8,128)(2,1)} fusion(bf16[2,8,512,128]{3,2,1,0:T(8,128)(2,1)} %param.18, s32[1024]{0:T(1024)S(1)} %pad_clamp_fusion.2), kind=kCustom, calls=%fused_computation.1.clone | custom fusion | bytes 8388672 | tf_op jit(solution)/shard_map/jit(_take)/gather | solution.py:59
  38.5 4.3 %select_bitcast_fusion.1 = (bf16[2,16,512,128]{3,2,0,1:T(8,128)(2,1)S(1)}, bf16[2,16,512,128]{3,2,0,1:T(8,128)(2,1)S(1)}) fusion(bf16[16,2,512,128]{3,2,1,0:T(8,128)(2,1)} %gather_fusion.4, pred[16]{0:T(512)(128)(4,1)S(1)} %compare_and_fusion, bf16[16,2,512,128]{3,2,1,0:T(8,128)(2,1)} %gather_fusion.5), kind=kLoop, calls=%fused_computation.49 | loop fusion | flops 4194304 | bytes 16777232 | tf_op jit(solution)/shard_map/jit(_take)/select_n | solution.py:58
  47.6 7.6 %maximum_select_fusion = bf16[32,512,256]{2,1,0:T(8,128)(2,1)} fusion(bf16[32,512,128]{2,1,0:T(8,128)(2,1)} %bitcast.168, bf16[32,512,128]{2,1,0:T(8,128)(2,1)} %bitcast.167, pred[32]{0:T(512)(128)(4,1)S(1)} %broadcast_in_dim.79), kind=kLoop, calls=%fused_computation.45 | loop fusion | flops 20971520 | bytes 16777248 | tf_op jit(solution)/shard_map/jit(_where)/select_n | solution.py:61
  55.3 5.0 %all-to-all-start = ((bf16[32,512,256]{2,1,0:T(8,128)(2,1)}), bf16[32,512,256]{2,1,0:T(8,128)(2,1)}, u32[]{:S(2)}, u32[]{:S(2)}) async-start(bf16[32,512,256]{2,1,0:T(8,128)(2,1)} %maximum_select_fusion), calls=%async_computation | async-start | bytes 16777216 | tf_op jit(solution)/shard_map/all_to_all | solution.py:65
  60.7 2.4 copy.63
  64.2 3.5 copy.65
  67.7 2.9 copy.45
  70.6 4.2 %reshape_squeeze.18 = bf16[1216,1024]{1,0:T(8,128)(2,1)} reshape(bf16[1,2,8,76,1024]{4,3,2,1,0:T(8,128)(2,1)} %copy.45) | data formatting | bytes 4980736 | tf_op jit(solution)/shard_map/reshape;squeeze | solution.py:73
  74.8 9.5 %convolution_convert_fusion = bf16[2048,1216]{0,1:T(8,128)(2,1)} fusion(bf16[1216,1024]{1,0:T(8,128)(2,1)} %reshape_squeeze.18, bf16[1024,2048]{1,0:T(8,128)(2,1)} %bitcast.178), kind=kOutput, calls=%fused_computation.46 | convolution fusion | flops 5102764032 | bytes 11665408 | tf_op jit(solution)/shard_map/dot_general | solution.py:79
  88.5 155.8 %all-to-all-done = bf16[32,512,256]{2,1,0:T(8,128)(2,1)} async-done(((bf16[32,512,256]{2,1,0:T(8,128)(2,1)}), bf16[32,512,256]{2,1,0:T(8,128)(2,1)}, u32[]{:S(2)}, u32[]{:S(2)}) %all-to-all-start) | async-done | bytes 8388640 | tf_op jit(solution)/shard_map/all_to_all | solution.py:65
  244.3 6.1 %gather_fusion.2 = bf16[16,512,256]{2,1,0:T(8,128)(2,1)} fusion(bf16[32,512,256]{2,1,0:T(8,128)(2,1)} %all-to-all-done, s32[1024]{0:T(1024)S(1)} %pad_clamp_fusion), kind=kCustom, calls=%fused_computation.4 | custom fusion | bytes 8388672 | tf_op jit(solution)/shard_map/gather | solution.py:72
  250.4 13.6 %scatter_custom_fusion = bf16[8192,256]{1,0:T(8,128)(2,1)} fusion(bf16[8192,256]{1,0:T(8,128)(2,1)} %bitcast.169, s32[1216]{0:T(1024)S(1)} %fusion.31, bf16[256,1216]{0,1:T(8,128)(2,1)} %reduce-scatter.2.cloned.1.call-done), kind=kCustom, calls=%fused_computation.58 | custom fusion | bytes 4816896 | tf_op jit(solution)/shard_map/scatter | solution.py:88
  264.0 4.0 slice_bitcast_fusion.1
  269.5 2.7 pad_maximum_fusion.1
  272.3 59.2 %while.24 = (s32[]{:T(128)}, bf16[2,128,1024]{2,1,0:T(8,128)(2,1)S(1)}, s32[2]{0:T(128)S(1)}, bf16[2,128,1024]{2,1,0:T(8,128)(2,1)S(1)}, bf16[4352,128]{1,0:T(8,...) while((s32[]{:T(128)}, bf16[2,128,1024]{2,1,0:T(8,128)(2,1)S(1)}, s32[2]{0:T(128)S(1)}, ...), condition=%wide.region_9.11_spmd, body=%wide.region_6.10_spmd.sunk | while | flops 2336430592 | bytes 60620388 | solution.py:103
  274.2 8.1 %fusion.54 = (f32[8,128]{1,0:T(8,128)S(1)}, f32[128,8,4352]{2,0,1:T(8,128)}) fusion(pred[128,4352]{1,0:T(8,128)(4,1)S(1)} %compare_or_fusion.4, bf16[128,8,128]{0,2,1:T(8,128)(2,1)S(1)} %bitcast.165, bf16[4352,128]{1,0:T(8,128)(2,1)S(1)} %get-tuple-element.363), kind=kOutput, calls=%fused_computation.11.clone.1 | convolution fusion | flops 1154219008 | bytes 19763200 | tf_op jit(solution)/shard_map/while/body/eval_jaxpr/qkgd,nkd->kgqn/dot_general | solution.py:17
  282.3 10.4 %fusion.55 = f32[8,128]{1,0:T(8,128)S(1)} fusion(f32[128,8,4352]{2,0,1:T(8,128)} %get-tuple-element.314, f32[8,128]{1,0:T(8,128)S(1)} %get-tuple-element.315, pred[128,4352]{1,0:T(8,128)(4,1)S(1)} %compare_or_fusion.4), kind=kLoop, calls=%fused_computation.10.clone.1 | loop fusion | flops 17824768 | bytes 18391040 | tf_op jit(solution)/shard_map/while/body/eval_jaxpr/reduce_sum | solution.py:25
  292.7 9.0 %fusion.56 = bf16[8,128,128]{1,2,0:T(8,128)(2,1)S(1)} fusion(f32[8,128]{1,0:T(8,128)S(1)} %fusion.55, f32[8,128]{1,0:T(8,128)S(1)} %get-tuple-element.315, f32[128,8,4352]{2,0,1:T(8,128)} %get-tuple-element.314, pred[128,4352]{1,0:T(8,128)(4,1)S(1)} %compare_or_fusion.4, bf16[4352,128]{0,1:T(8,128)(2,1)} %get-tuple-element.364), kind=kOutput, calls=%fused_computation.15.clone.1 | convolution fusion | flops 1163264000 | bytes 19767296 | tf_op jit(solution)/shard_map/while/body/eval_jaxpr/kgqn,nkd->qkgd/dot_general | solution.py:26
  303.8 8.1 %fusion.54 = (f32[8,128]{1,0:T(8,128)S(1)}, f32[128,8,4352]{2,0,1:T(8,128)}) fusion(pred[128,4352]{1,0:T(8,128)(4,1)S(1)} %compare_or_fusion.4, bf16[128,8,128]{0,2,1:T(8,128)(2,1)S(1)} %bitcast.165, bf16[4352,128]{1,0:T(8,128)(2,1)S(1)} %get-tuple-element.363), kind=kOutput, calls=%fused_computation.11.clone.1 | convolution fusion | flops 1154219008 | bytes 19763200 | tf_op jit(solution)/shard_map/while/body/eval_jaxpr/qkgd,nkd->kgqn/dot_general | solution.py:17
  311.9 10.4 %fusion.55 = f32[8,128]{1,0:T(8,128)S(1)} fusion(f32[128,8,4352]{2,0,1:T(8,128)} %get-tuple-element.314, f32[8,128]{1,0:T(8,128)S(1)} %get-tuple-element.315, pred[128,4352]{1,0:T(8,128)(4,1)S(1)} %compare_or_fusion.4), kind=kLoop, calls=%fused_computation.10.clone.1 | loop fusion | flops 17824768 | bytes 18391040 | tf_op jit(solution)/shard_map/while/body/eval_jaxpr/reduce_sum | solution.py:25
  322.3 9.0 %fusion.56 = bf16[8,128,128]{1,2,0:T(8,128)(2,1)S(1)} fusion(f32[8,128]{1,0:T(8,128)S(1)} %fusion.55, f32[8,128]{1,0:T(8,128)S(1)} %get-tuple-element.315, f32[128,8,4352]{2,0,1:T(8,128)} %get-tuple-element.314, pred[128,4352]{1,0:T(8,128)(4,1)S(1)} %compare_or_fusion.4, bf16[4352,128]{0,1:T(8,128)(2,1)} %get-tuple-element.364), kind=kOutput, calls=%fused_computation.15.clone.1 | convolution fusion | flops 1163264000 | bytes 19767296 | tf_op jit(solution)/shard_map/while/body/eval_jaxpr/kgqn,nkd->qkgd/dot_general | solution.py:26
  331.5 2.5 copy.61
  334.0 2.3 pad_maximum_fusion.4
  336.4 59.4 %while.25 = (s32[]{:T(128)}, bf16[2,128,1024]{2,1,0:T(8,128)(2,1)S(1)}, s32[2]{0:T(128)S(1)}, bf16[2,128,1024]{2,1,0:T(8,128)(2,1)S(1)}, bf16[4352,128]{1,0:T(8,...) while((s32[]{:T(128)}, bf16[2,128,1024]{2,1,0:T(8,128)(2,1)S(1)}, s32[2]{0:T(128)S(1)}, ...), condition=%wide.region_13.15_spmd, body=%wide.region_10.14_spmd.sunk | while | flops 2336430592 | bytes 60620388 | solution.py:103
  338.5 8.1 %fusion.60 = (f32[8,128]{1,0:T(8,128)S(1)}, f32[128,8,4352]{2,0,1:T(8,128)}) fusion(pred[128,4352]{1,0:T(8,128)(4,1)S(1)} %compare_or_fusion.5, bf16[128,8,128]{0,2,1:T(8,128)(2,1)S(1)} %bitcast.166, bf16[4352,128]{1,0:T(8,128)(2,1)S(1)} %get-tuple-element.342), kind=kOutput, calls=%fused_computation.30.clone.1 | convolution fusion | flops 1154219008 | bytes 19763200 | tf_op jit(solution)/shard_map/while/body/eval_jaxpr/qkgd,nkd->kgqn/dot_general | solution.py:17
  346.6 10.4 %fusion.61 = f32[8,128]{1,0:T(8,128)S(1)} fusion(f32[128,8,4352]{2,0,1:T(8,128)} %get-tuple-element.322, f32[8,128]{1,0:T(8,128)S(1)} %get-tuple-element.323, pred[128,4352]{1,0:T(8,128)(4,1)S(1)} %compare_or_fusion.5), kind=kLoop, calls=%fused_computation.29.clone.1 | loop fusion | flops 17824768 | bytes 18391040 | tf_op jit(solution)/shard_map/while/body/eval_jaxpr/reduce_sum | solution.py:25
  357.0 9.0 %fusion.62 = bf16[8,128,128]{1,2,0:T(8,128)(2,1)S(1)} fusion(f32[8,128]{1,0:T(8,128)S(1)} %fusion.61, f32[8,128]{1,0:T(8,128)S(1)} %get-tuple-element.323, f32[128,8,4352]{2,0,1:T(8,128)} %get-tuple-element.322, pred[128,4352]{1,0:T(8,128)(4,1)S(1)} %compare_or_fusion.5, bf16[4352,128]{0,1:T(8,128)(2,1)} %get-tuple-element.343), kind=kOutput, calls=%fused_computation.34.clone.1 | convolution fusion | flops 1163264000 | bytes 19767296 | tf_op jit(solution)/shard_map/while/body/eval_jaxpr/kgqn,nkd->qkgd/dot_general | solution.py:26
  368.1 8.1 %fusion.60 = (f32[8,128]{1,0:T(8,128)S(1)}, f32[128,8,4352]{2,0,1:T(8,128)}) fusion(pred[128,4352]{1,0:T(8,128)(4,1)S(1)} %compare_or_fusion.5, bf16[128,8,128]{0,2,1:T(8,128)(2,1)S(1)} %bitcast.166, bf16[4352,128]{1,0:T(8,128)(2,1)S(1)} %get-tuple-element.342), kind=kOutput, calls=%fused_computation.30.clone.1 | convolution fusion | flops 1154219008 | bytes 19763200 | tf_op jit(solution)/shard_map/while/body/eval_jaxpr/qkgd,nkd->kgqn/dot_general | solution.py:17
  376.2 10.4 %fusion.61 = f32[8,128]{1,0:T(8,128)S(1)} fusion(f32[128,8,4352]{2,0,1:T(8,128)} %get-tuple-element.322, f32[8,128]{1,0:T(8,128)S(1)} %get-tuple-element.323, pred[128,4352]{1,0:T(8,128)(4,1)S(1)} %compare_or_fusion.5), kind=kLoop, calls=%fused_computation.29.clone.1 | loop fusion | flops 17824768 | bytes 18391040 | tf_op jit(solution)/shard_map/while/body/eval_jaxpr/reduce_sum | solution.py:25
  386.6 9.0 %fusion.62 = bf16[8,128,128]{1,2,0:T(8,128)(2,1)S(1)} fusion(f32[8,128]{1,0:T(8,128)S(1)} %fusion.61, f32[8,128]{1,0:T(8,128)S(1)} %get-tuple-element.323, f32[128,8,4352]{2,0,1:T(8,128)} %get-tuple-element.322, pred[128,4352]{1,0:T(8,128)(4,1)S(1)} %compare_or_fusion.5, bf16[4352,128]{0,1:T(8,128)(2,1)} %get-tuple-element.343), kind=kOutput, calls=%fused_computation.34.clone.1 | convolution fusion | flops 1163264000 | bytes 19767296 | tf_op jit(solution)/shard_map/while/body/eval_jaxpr/kgqn,nkd->qkgd/dot_general | solution.py:26
  (111 shorter events, 25.2 us)
Async XLA Ops:
  6.5 24.3 %copy-start = (bf16[2,8,512,128]{3,2,1,0:T(8,128)(2,1)S(1)}, bf16[2,8,512,128]{3,2,1,0:T(8,128)(2,1)}, u32[]{:S(2)}) copy-start(bf16[2,8,512,128]{3,2,1,0:T(8,128)(2,1)} %param.17) | copy-start | bytes 6291460
  6.5 21.8 %copy-start.2 = (s32[256]{0:T(256)S(1)}, s32[256]{0:T(256)}, u32[]{:S(2)}) copy-start(s32[256]{0:T(256)} %param.20) | copy-start | bytes 3076
  55.3 189.0 %all-to-all-start = ((bf16[32,512,256]{2,1,0:T(8,128)(2,1)}), bf16[32,512,256]{2,1,0:T(8,128)(2,1)}, u32[]{:S(2)}, u32[]{:S(2)}) async-start(bf16[32,512,256]{2,1,0:T(8,128)(2,1)} %maximum_select_fusion), calls=%async_computation | async-start | bytes 16777216 | tf_op jit(solution)/shard_map/all_to_all | solution.py:65
  60.2 190.2 %reduce-scatter.2.cloned.1.call-start = ((), (), s32[]{:S(2)}) async-start(), calls=%async_computation.2 | async-start | bytes 5603328 | tf_op jit(solution)/shard_map/reduce_scatter | solution.py:78
  60.7 2.4 copy-start.6
  64.2 3.5 copy-start.5
  84.3 0.7 copy-start.13
  84.3 1.6 copy-start.12
  84.3 2.5 copy-start.10
  84.3 3.3 copy-start.11
  84.3 3.3 copy-start.8
  272.3 61.7 %copy-start.9 = (bf16[1,1,256,128]{2,3,1,0:T(8,128)(2,1)S(1)}, bf16[1,1,256,128]{2,3,1,0:T(8,128)(2,1)}, u32[]{:S(2)}) copy-start(bf16[1,1,256,128]{2,3,1,0:T(8,128)(2,1)} %copy.62) | copy-start | bytes 196612
  331.5 4.8 %copy-start.7 = (bf16[2,128,1024]{2,1,0:T(8,128)(2,1)}, bf16[2,128,1024]{2,1,0:T(8,128)(2,1)S(1)}, u32[]{:S(2)}) copy-start(bf16[2,128,1024]{2,1,0:T(8,128)(2,1)S(1)} %get-tuple-element.160) | copy-start | bytes 1572868
  331.5 4.9 %copy-start.3 = (bf16[4352,128]{1,0:T(8,128)(2,1)S(1)}, bf16[4352,128]{1,0:T(8,128)(2,1)}, u32[]{:S(2)}) copy-start(bf16[4352,128]{1,0:T(8,128)(2,1)} %get-tuple-element.328) | copy-start | bytes 3342340
  331.5 4.9 %copy-start.4 = (bf16[1,1,256,1024]{3,2,1,0:T(8,128)(2,1)S(1)}, bf16[1,1,256,1024]{3,2,1,0:T(8,128)(2,1)}, u32[]{:S(2)}) copy-start(bf16[1,1,256,1024]{3,2,1,0:T(8,128)(2,1)} %get-tuple-element.233) | copy-start | bytes 1572868
  395.8 2.3 copy-start.1
Sparse Core Ops, SparseCore 0:
  84.5 134.9 reduce-scatter.1
where the time goes:
time: 412 us; the launch traced here: 405 us
  waiting for transfers between devices  156 us (38%)
  matrix products  77.8 us (19%)
  other arithmetic  66.3 us (16%)
  local copies, waits for them, and re-layouts  63.6 us (15%)
  blocking collectives  21.7 us (5%)
  between operations  14 us (3%)
  starting transfers between devices  5.46 us (1%)
    all_to_all x1, waiting for transfers between devices, on_device(): lax.all_to_all(outgoing.reshape(owners, clen, 2 * width), ('section', 'dp...  156 us
    reduce_sum x4, other arithmetic, attend_block(): probs = (expo / jnp.sum(expo, axis=-1, keepdims=True)).astype(jnp.bfloat16)  41.6 us
    dot_general x4, matrix products, attend_block(): jnp.einsum('kgqn,nkd->qkgd', probs, valued, preferred_element_type=jnp.fl...  35.9 us
    dot_general x4, matrix products, attend_block(): jnp.einsum('qkgd,nkd->kgqn', queried, keyed, preferred_element_type=jnp.f...  32.4 us
    all_gather x1, blocking collectives, on_device(): every_list = lax.all_gather(span_ids, 'dp', axis=0, tiled=True)  21.7 us
    scatter x1, local copies, waits for them, and re-layouts, on_device(): fetched.at[flat].set(fresh).reshape(req_dev, topk * clen, 2 * width)  13.6 us
    unnamed x35, local copies, waits for them, and re-layouts  13.4 us
    dot_general x1, matrix products, on_device(): lax.dot_general(joined, rows, (((0,), (1,)), ((), ())), preferred_element...  9.53 us
  transfers between devices with their start and end apart: 2, of which 1 were waited for; matrix products, arithmetic and copies ran while one was open for 8% of the time, Pallas kernels for 0%

commit v1 on v0

v1 whole, which is shorter than its diff:
```python
import functools

import jax
import jax.numpy as jnp
from jax import lax
from jax.experimental import pallas as pl
from jax.experimental.pallas import tpu as pltpu
from jax.sharding import PartitionSpec as P

HD = 128
TILE = 16
MIB = 1 << 20
LOG2E = 1.4426950408889634


def ceil_to(n, m):
    return -(-n // m) * m


def compact_kernel(ids_ref, rows_ref, ck_ref, cv_ref, out_ref, *, kept):
    layers, _, clen, width = ck_ref.shape
    padded = out_ref.shape[2]
    rr = rows_ref.shape[1]
    rows = rows_ref[pl.ds(lax.rem(ids_ref[pl.program_id(0)], 8), 1), :]
    hit = (lax.broadcasted_iota(jnp.int32, (clen, rr), 0) == rows).astype(jnp.bfloat16)
    gone = lax.dot_general(
        jnp.ones((8, rr), jnp.bfloat16), hit, (((1,), (1,)), ((), ())),
        preferred_element_type=jnp.float32,
    )
    keep = 1.0 - gone
    earlier = (
        lax.broadcasted_iota(jnp.int32, (clen, clen), 0)
        < lax.broadcasted_iota(jnp.int32, (clen, clen), 1)
    ).astype(jnp.bfloat16)
    rank = jnp.dot(keep.astype(jnp.bfloat16), earlier, preferred_element_type=jnp.float32)[:1]
    rank = jnp.where(keep[:1] > 0.5, rank.astype(jnp.int32), -1)
    target = lax.broadcasted_iota(jnp.int32, (padded, clen), 0)
    target = jnp.where(target < kept, target, 0)
    pick = (target == rank).astype(jnp.bfloat16)
    for layer in range(layers):
        both = jnp.concatenate([ck_ref[layer, 0], cv_ref[layer, 0]], axis=1)
        out_ref[layer, 0] = jnp.dot(
            pick, both, preferred_element_type=jnp.float32
        ).astype(out_ref.dtype)


def compact(ids, recompute_rows, cache_keys, cache_values, kept, padded):
    layers, spans, clen, width = cache_keys.shape
    rr = recompute_rows.shape[1]
    return pl.pallas_call(
        functools.partial(compact_kernel, kept=kept),
        grid_spec=pltpu.PrefetchScalarGridSpec(
            num_scalar_prefetch=1,
            grid=(spans,),
            in_specs=[
                pl.BlockSpec((8, rr), lambda i, ids: (ids[i] // 8, 0)),
                pl.BlockSpec((layers, 1, clen, width), lambda i, ids: (0, i, 0, 0)),
                pl.BlockSpec((layers, 1, clen, width), lambda i, ids: (0, i, 0, 0)),
            ],
            out_specs=pl.BlockSpec((layers, 1, padded, 2 * width), lambda i, ids: (0, i, 0, 0)),
        ),
        out_shape=jax.ShapeDtypeStruct((layers, spans, padded, 2 * width), jnp.bfloat16),
        compiler_params=pltpu.CompilerParams(vmem_limit_bytes=56 * MIB),
        cost_estimate=pl.CostEstimate(
            flops=2 * layers * spans * padded * clen * 2 * width,
            bytes_accessed=8 * layers * spans * clen * width,
            transcendentals=0,
        ),
        name="compact",
    )(ids, recompute_rows, cache_keys, cache_values)


def spread_kernel(local_ref, packed_ref, main_ref, rest_ref, sem, *, groups, cut):
    layers, _, padded, _ = packed_ref.shape

    def copies(g):
        made = []
        for layer in range(layers):
            dest = layer * groups + g
            made.append(
                pltpu.make_async_copy(
                    packed_ref.at[layer, local_ref[g], pl.ds(0, cut)],
                    main_ref.at[dest],
                    sem.at[0, dest],
                )
            )
            made.append(
                pltpu.make_async_copy(
                    packed_ref.at[layer, local_ref[g], pl.ds(cut, padded - cut)],
                    rest_ref.at[dest],
                    sem.at[1, dest],
                )
            )
        return made

    for g in range(groups):

        @pl.when(local_ref[g] >= 0)
        def _():
            for copy in copies(g):
                copy.start()

    for g in range(groups):

        @pl.when(local_ref[g] >= 0)
        def _():
            for copy in copies(g):
                copy.wait()


def spread(local, packed, cut):
    layers, spans, padded, wide = packed.shape
    groups = local.shape[0]
    dests = layers * groups
    return pl.pallas_call(
        functools.partial(spread_kernel, groups=groups, cut=cut),
        in_specs=[
            pl.BlockSpec(memory_space=pltpu.SMEM),
            pl.BlockSpec(memory_space=pltpu.VMEM),
        ],
        out_specs=[pl.BlockSpec(memory_space=pl.ANY), pl.BlockSpec(memory_space=pl.ANY)],
        out_shape=[
            jax.ShapeDtypeStruct((dests, cut, wide), jnp.bfloat16),
            jax.ShapeDtypeStruct((dests, padded - cut, wide), jnp.bfloat16),
        ],
        scratch_shapes=[pltpu.SemaphoreType.DMA((2, dests))],
        compiler_params=pltpu.CompilerParams(vmem_limit_bytes=56 * MIB),
        cost_estimate=pl.CostEstimate(
            flops=0, bytes_accessed=2 * (dests + layers * spans) * padded * wide, transcendentals=0
        ),
        name="spread",
    )(local, packed)


def project_kernel(hidden_ref, wk_ref, wv_ref, out_ref, rows_ref, *, rrows, slot):
    _, reqs, topk, _, _ = hidden_ref.shape

    @pl.when(pl.program_id(0) == 0)
    def _():
        for r in range(reqs):
            for j in range(topk):
                at = (r * topk + j) * slot
                rows_ref[at : at + rrows] = hidden_ref[0, r, j]
                if slot > rrows:
                    rows_ref[at + rrows : at + slot] = hidden_ref[0, r, j, : slot - rrows]

    weight = jnp.concatenate([wk_ref[0], wv_ref[0]], axis=1)
    out_ref[0] = jnp.dot(
        rows_ref[...], weight, preferred_element_type=jnp.float32
    ).astype(out_ref.dtype)


def project(hidden, w_key, w_value, slot, parts):
    _, reqs, topk, rrows, feats = hidden.shape
    spans = reqs * topk
    share = w_key.shape[2] // parts
    return pl.pallas_call(
        functools.partial(project_kernel, rrows=rrows, slot=slot),
        grid=(parts,),
        in_specs=[
            pl.BlockSpec(hidden.shape, lambda p: (0, 0, 0, 0, 0)),
            pl.BlockSpec((1, feats, share), lambda p: (0, 0, p)),
            pl.BlockSpec((1, feats, share), lambda p: (0, 0, p)),
        ],
        out_specs=pl.BlockSpec((1, spans * slot, 2 * share), lambda p: (p, 0, 0)),
        out_shape=jax.ShapeDtypeStruct((parts, spans * slot, 2 * share), jnp.bfloat16),
        scratch_shapes=[pltpu.VMEM((spans * slot, feats), jnp.bfloat16)],
        compiler_params=pltpu.CompilerParams(vmem_limit_bytes=56 * MIB),
        cost_estimate=pl.CostEstimate(
            flops=4 * parts * spans * slot * feats * share,
            bytes_accessed=2 * spans * rrows * feats + 4 * parts * (feats + spans * slot) * share,
            transcendentals=0,
        ),
        name="project",
    )(hidden, w_key, w_value)


def attend_step(q_ref, key_ref, wide_ref, acc_ref, top_ref, first, causal):
    heads = acc_ref.shape[0]
    qlen = acc_ref.shape[1]
    count = key_ref.shape[0]
    factor = LOG2E / (HD ** 0.5)

    def one_head(h):
        q = q_ref[:, h * HD : (h + 1) * HD]
        scores = lax.dot_general(
            q, key_ref[...], (((1,), (1,)), ((), ())), preferred_element_type=jnp.float32
        )
        if causal is not None:
            scores = jnp.concatenate(
                [scores[:, : count - qlen], jnp.where(causal, scores[:, count - qlen :], -1e30)],
                axis=1,
            )
        best = jnp.max(scores, axis=1, keepdims=True) * factor
        if first:
            top = best
        else:
            old = top_ref[h][:, :1]
            top = jnp.maximum(old, best)
        probs = jnp.exp2(scores * factor - top).astype(jnp.bfloat16)
        part = jnp.dot(probs, wide_ref[...], preferred_element_type=jnp.float32)
        if first:
            acc_ref[h] = part
        else:
            acc_ref[h] = acc_ref[h] * jnp.exp2(old - top) + part
        top_ref[h] = jnp.broadcast_to(top, (qlen, HD))

    for h in range(heads):
        one_head(h)


def gather_keys(blocks, key_ref, wide_ref, at, kept):
    rows = blocks[0].shape[1]
    real = lax.broadcasted_iota(jnp.int32, (rows, HD), 0) < kept
    for ref in blocks:
        key_ref[at : at + rows] = ref[0, :, :HD]
        value = ref[0, :, HD:]
        if kept < rows:
            value = jnp.where(real, value, 0).astype(jnp.bfloat16)
        wide_ref[at : at + rows, :HD] = value
        wide_ref[at : at + rows, HD:] = real.astype(jnp.bfloat16)
        at += rows


def main_kernel(place_ref, q_ref, fresh_ref, nk_ref, nv_ref, *rest, rrows, slot):
    acc_ref, top_ref, key_ref, wide_ref = rest[-4:]
    blocks = rest[:-4]
    rows = blocks[0].shape[1]
    fresh_rows = fresh_ref.shape[0]
    qlen = nk_ref.shape[2]
    gather_keys(blocks, key_ref, wide_ref, 0, rows)
    at = rows * len(blocks)
    end = at + fresh_rows
    real = lax.broadcasted_iota(jnp.int32, (fresh_rows, HD), 0) % slot < rrows
    key_ref[at:end] = fresh_ref[:, :HD]
    wide_ref[at:end, :HD] = jnp.where(real, fresh_ref[:, HD:], 0).astype(jnp.bfloat16)
    wide_ref[at:end, HD:] = real.astype(jnp.bfloat16)
    key_ref[end:] = nk_ref[0, 0]
    wide_ref[end:, :HD] = nv_ref[0, 0]
    wide_ref[end:, HD:] = jnp.ones((qlen, HD), jnp.bfloat16)
    causal = lax.broadcasted_iota(jnp.int32, (qlen, qlen), 0) >= lax.broadcasted_iota(
        jnp.int32, (qlen, qlen), 1
    )
    attend_step(q_ref.at[0, 0], key_ref, wide_ref, acc_ref.at[0], top_ref.at[0], True, causal)


def block_specs(rows, topk):
    return [
        pl.BlockSpec((1, rows, 2 * HD), lambda r, at, j=j: (at[r * topk + j], 0, 0))
        for j in range(topk)
    ]


def attend_main(place, queries, fresh, query_keys, query_values, arrived, rrows, slot):
    _, reqs, qlen, feats = queries.shape
    heads = feats // HD
    rows = arrived.shape[1]
    topk = place.shape[0] // reqs
    fresh_rows = fresh.shape[0] // reqs
    count = topk * rows + fresh_rows + qlen
    return pl.pallas_call(
        functools.partial(main_kernel, rrows=rrows, slot=slot),
        grid_spec=pltpu.PrefetchScalarGridSpec(
            num_scalar_prefetch=1,
            grid=(reqs,),
            in_specs=[
                pl.BlockSpec((1, 1, qlen, feats), lambda r, at: (0, r, 0, 0)),
                pl.BlockSpec((fresh_rows, 2 * HD), lambda r, at: (r, 0)),
                pl.BlockSpec((1, 1, qlen, HD), lambda r, at: (0, r, 0, 0)),
                pl.BlockSpec((1, 1, qlen, HD), lambda r, at: (0, r, 0, 0)),
            ]
            + block_specs(rows, topk),
            out_specs=[
                pl.BlockSpec((1, heads, qlen, 2 * HD), lambda r, at: (r, 0, 0, 0)),
                pl.BlockSpec((1, heads, qlen, HD), lambda r, at: (r, 0, 0, 0)),
            ],
            scratch_shapes=[
                pltpu.VMEM((count, HD), jnp.bfloat16),
                pltpu.VMEM((count, 2 * HD), jnp.bfloat16),
            ],
        ),
        out_shape=[
            jax.ShapeDtypeStruct((reqs, heads, qlen, 2 * HD), jnp.float32),
            jax.ShapeDtypeStruct((reqs, heads, qlen, HD), jnp.float32),
        ],
        compiler_params=pltpu.CompilerParams(vmem_limit_bytes=56 * MIB),
        cost_estimate=pl.CostEstimate(
            flops=6 * reqs * heads * qlen * count * HD,
            bytes_accessed=4 * reqs * count * HD + 12 * reqs * heads * qlen * HD,
            transcendentals=reqs * heads * qlen * count,
        ),
        name="attend_main",
    )(place, queries, fresh, query_keys, query_values, *([arrived] * topk))


def last_kernel(place_ref, q_ref, acc_in, top_in, *rest, kept):
    out_ref, acc_ref, top_ref, key_ref, wide_ref = rest[-5:]
    gather_keys(rest[:-5], key_ref, wide_ref, 0, kept)
    acc_ref[...] = acc_in[0]
    top_ref[...] = top_in[0]
    attend_step(q_ref.at[0, 0], key_ref, wide_ref, acc_ref, top_ref, False, None)
    for h in range(acc_ref.shape[0]):
        total = acc_ref[h]
        out_ref[0, 0, :, h * HD : (h + 1) * HD] = (total[:, :HD] / total[:, HD:]).astype(
            out_ref.dtype
        )


def attend_last(place, queries, acc, top, arrived, kept):
    _, reqs, qlen, feats = queries.shape
    heads = feats // HD
    rows = arrived.shape[1]
    topk = place.shape[0] // reqs
    count = topk * rows
    return pl.pallas_call(
        functools.partial(last_kernel, kept=kept),
        grid_spec=pltpu.PrefetchScalarGridSpec(
            num_scalar_prefetch=1,
            grid=(reqs,),
            in_specs=[
                pl.BlockSpec((1, 1, qlen, feats), lambda r, at: (0, r, 0, 0)),
                pl.BlockSpec((1, heads, qlen, 2 * HD), lambda r, at: (r, 0, 0, 0)),
                pl.BlockSpec((1, heads, qlen, HD), lambda r, at: (r, 0, 0, 0)),
            ]
            + block_specs(rows, topk),
            out_specs=pl.BlockSpec((1, 1, qlen, feats), lambda r, at: (0, r, 0, 0)),
            scratch_shapes=[
                pltpu.VMEM((heads, qlen, 2 * HD), jnp.float32),
                pltpu.VMEM((heads, qlen, HD), jnp.float32),
                pltpu.VMEM((count, HD), jnp.bfloat16),
                pltpu.VMEM((count, 2 * HD), jnp.bfloat16),
            ],
        ),
        out_shape=jax.ShapeDtypeStruct(queries.shape, jnp.bfloat16),
        compiler_params=pltpu.CompilerParams(vmem_limit_bytes=56 * MIB),
        cost_estimate=pl.CostEstimate(
            flops=6 * reqs * heads * qlen * count * HD,
            bytes_accessed=4 * reqs * count * HD + 12 * reqs * heads * qlen * HD,
            transcendentals=reqs * heads * qlen * count,
        ),
        name="attend_last",
    )(place, queries, acc, top, *([arrived] * topk))


def on_device(
    cache_keys,
    cache_values,
    span_ids,
    owner_slot,
    recompute_rows,
    hidden,
    w_key,
    w_value,
    queries,
    query_keys,
    query_values,
):
    sections = lax.axis_size("section")
    groups = lax.axis_size("dp")
    parts = lax.axis_size("tensor")
    per_owner = cache_keys.shape[1]
    clen = cache_keys.shape[2]
    req_dev, topk = span_ids.shape
    rrows = hidden.shape[3]
    kept = clen - rrows
    cut = kept // HD * HD
    padded = ceil_to(kept, 64)
    slot = ceil_to(rrows, TILE)
    myself = lax.axis_index("section") * groups + lax.axis_index("dp")

    own_slot = owner_slot[span_ids].reshape(req_dev * topk)
    every_slot = lax.all_to_all(
        jnp.broadcast_to(own_slot[None], (groups, req_dev * topk)), "dp", 0, 0
    )

    here = myself * per_owner + jnp.arange(per_owner, dtype=jnp.int32)
    held = owner_slot[None, :] == here[:, None]
    ids = jnp.sum(
        jnp.where(held, jnp.arange(owner_slot.shape[0], dtype=jnp.int32)[None], 0), axis=1
    )
    packed = compact(ids, recompute_rows, cache_keys, cache_values, kept, padded)

    partial = project(hidden, w_key, w_value, slot, parts)

    mine = every_slot // per_owner == myself
    local = jnp.max(jnp.where(mine, every_slot % per_owner, -1), axis=1)
    main, rest = spread(local, packed, cut)
    arrived = lax.all_to_all(main, ("section", "dp"), 0, 0, tiled=True)
    fresh = lax.psum_scatter(
        partial.reshape(parts * req_dev * topk * slot, -1),
        "tensor",
        scatter_dimension=0,
        tiled=True,
    )
    rest, arrived = lax.optimization_barrier((rest, arrived))
    arrived_rest = lax.all_to_all(rest, ("section", "dp"), 0, 0, tiled=True)

    place = own_slot // per_owner
    acc, top = attend_main(
        place, queries, fresh, query_keys, query_values, arrived, rrows, slot
    )
    return attend_last(place, queries, acc, top, arrived_rest, kept - cut)


def solution(mesh):
    in_specs = (
        P(None, ("section", "dp"), None, "tensor"),
        P(None, ("section", "dp"), None, "tensor"),
        P("dp", None),
        P(),
        P(),
        P("section", "dp", None, None, "tensor"),
        P("section", "tensor", None),
        P("section", "tensor", None),
        P("section", "dp", None, "tensor"),
        P("section", "dp", None, "tensor"),
        P("section", "dp", None, "tensor"),
    )
    out_specs = P("section", "dp", None, "tensor")
    return jax.shard_map(
        on_device, mesh=mesh, in_specs=in_specs, out_specs=out_specs, check_vma=False
    )
```

time: 412 us -> 242 us (0.59); the launches traced: 405 us -> 242 us
  matrix products: 77.8 us -> 0 us
  Pallas kernels: 0 us -> 64.7 us
  other arithmetic: 66.3 us -> 3.27 us
  local copies, waits for them, and re-layouts: 63.6 us -> 7.47 us
  waiting for transfers between devices: 156 us -> 125 us
  starting transfers between devices: 5.46 us -> 27.8 us
  blocking collectives: 21.7 us -> 0 us
    dot_general x9 -> x0, matrix products: 77.8 us -> none  [the longest x4 35.9 us: attend_block(): jnp.einsum('kgqn,nkd->qkgd', probs, valued, preferred_element_type=jnp.fl...]
    pallas_call x0 -> x5, Pallas kernels: none -> 64.7 us  [the longest x1 30.2 us: attend_main(): pl.pallas_call(functools.partial(main_kernel, rrows=rrows, slot=slot), gr...]
    reduce_sum x6 -> x1, other arithmetic: 41.8 us -> 1.34 us  [on_device(): jnp.sum(jnp.where(held, jnp.arange(owner_slot.shape[0], dtype=jnp.int32)[...]
    all_to_all x1 -> x3, waiting for transfers between devices: 156 us -> 125 us  [the longest x1 125 us: on_device(): arrived = lax.all_to_all(main, ('section', 'dp'), 0, 0, tiled=True)]
    all_to_all x1 -> x3, starting transfers between devices: 4.95 us -> 27.7 us  [the longest x1 9.98 us: on_device(): lax.all_to_all(jnp.broadcast_to(own_slot[None], (groups, req_dev * topk))...]
    all_gather x1 -> x0, blocking collectives: 21.7 us -> none  [on_device(): every_list = lax.all_gather(span_ids, 'dp', axis=0, tiled=True)]
    gather x8 -> x1, local copies, waits for them, and re-layouts: 17.1 us -> 1.34 us  [on_device(): own_slot = owner_slot[span_ids].reshape(req_dev * topk)]
    scatter x1 -> x0, local copies, waits for them, and re-layouts: 13.6 us -> none  [on_device(): fetched.at[flat].set(fresh).reshape(req_dev, topk * clen, 2 * width)]
  transfers between devices with their start and end apart: 2 -> 4, of which waited for: 1 -> 1; matrix products, arithmetic and copies ran while one was open for 8% -> 3% of each run, Pallas kernels for 0% -> 21%
where the time goes in v1:
time: 242 us
  waiting for transfers between devices  125 us (52%)
  Pallas kernels  64.7 us (27%)
  starting transfers between devices  27.8 us (11%)
  between operations  13.5 us (6%)
  local copies, waits for them, and re-layouts  7.47 us (3%)
  other arithmetic  3.27 us (1%)
    all_to_all x1, waiting for transfers between devices, on_device(): arrived = lax.all_to_all(main, ('section', 'dp'), 0, 0, tiled=True)  125 us
    pallas_call x1, Pallas kernels, attend_main(): pl.pallas_call(functools.partial(main_kernel, rrows=rrows, slot=slot), gr...  30.2 us
    pallas_call x1, Pallas kernels, project(): pl.pallas_call(functools.partial(project_kernel, rrows=rrows, slot=slot),...  11.3 us
    all_to_all x1, starting transfers between devices, on_device(): lax.all_to_all(jnp.broadcast_to(own_slot[None], (groups, req_dev * topk))...  9.98 us
    pallas_call x1, Pallas kernels, compact(): pl.pallas_call(functools.partial(compact_kernel, kept=kept), grid_spec=pl...  9.74 us
    all_to_all x1, starting transfers between devices, on_device(): arrived_rest = lax.all_to_all(rest, ('section', 'dp'), 0, 0, tiled=True)  8.99 us
    all_to_all x1, starting transfers between devices, on_device(): arrived = lax.all_to_all(main, ('section', 'dp'), 0, 0, tiled=True)  8.76 us
    pallas_call x1, Pallas kernels, attend_last(): pl.pallas_call(functools.partial(last_kernel, kept=kept), grid_spec=pltpu...  8.57 us
  transfers between devices with their start and end apart: 4, of which 1 were waited for; matrix products, arithmetic and copies ran while one was open for 3% of the time, Pallas kernels for 21%

profile of v1, /device:TPU:1, one launch (start us, length us, event | category | flops | bytes accessed | tf_op | source)
XLA Modules:
  0.0 241.9 jit_solution(9742664784031261514)
XLA Ops:
  6.5 0.7 compare_select_fusion
  7.2 0.1 reshape.23
  7.3 1.3 gather_fusion
  8.7 0.6 broadcast_in_dim.26
  9.3 10.0 %all-to-all-start = ((s32[16,1,16]{2,1,0:T(1,128)}), s32[16,1,16]{2,1,0:T(1,128)S(1)}, u32[]{:S(2)}, u32[]{:S(2)}) async-start(s32[16,1,16]{2,1,0:T(1,128)} %broadcast_in_dim.26), calls=%async_computation.1 | async-start | bytes 16384 | tf_op jit(solution)/shard_map/all_to_all | solution.py:372
  19.2 1.3 select_reduce_fusion.ids_ref
  20.6 1.6 copy.19.rows_ref
  22.2 9.7 %compact.1.packed_ref = bf16[2,8,448,256]{3,2,1,0:T(8,128)(2,1)} custom-call(s32[8]{0:T(128)} %select_reduce_fusion.ids_ref, s32[256,76]{1,0:T(8,128)} %copy.19.rows_ref, bf16[2,8,512,128]{3,2,1,0:T(8,128)(2,1)} %ck_ref.1, bf16[2,8,512,128]{3,2,1,0:T(8,128)(2,1)} %cv_ref.1), custom_call_target="tpu_custom_call" | custom-call | flops 1879048192 | bytes 8388608 | tf_op jit(solution)/shard_map/compact/pallas_call | solution.py:50
  32.0 0.0 all-to-all-done
  32.0 0.7 fusion.2.local_ref
  32.7 4.9 %spread.1 = (bf16[32,384,256]{2,1,0:T(8,128)(2,1)}, bf16[32,64,256]{2,1,0:T(8,128)(2,1)}) custom-call(s32[16]{0:T(128)} %fusion.2.local_ref, bf16[2,8,448,256]{3,2,1,0:T(8,128)(2,1)} %compact.1.packed_ref), custom_call_target="tpu_custom_call" | custom-call | bytes 11010048 | tf_op jit(solution)/shard_map/spread/pallas_call | solution.py:115
  37.5 0.0 copy-start.1
  37.6 8.8 %all-to-all-start.1 = ((bf16[32,384,256]{2,1,0:T(8,128)(2,1)}), bf16[32,384,256]{2,1,0:T(8,128)(2,1)}, u32[]{:S(2)}, u32[]{:S(2)}) async-start(bf16[32,384,256]{2,1,0:T(8,128)(2,1)} %get-tuple-element.12), calls=%async_computation.2 | async-start | bytes 12582912 | tf_op jit(solution)/shard_map/all_to_all | solution.py:388
  46.3 0.0 reduce-scatter.2.cloned.1.call-start
  46.4 0.0 copy-done.1
  46.4 2.8 %copy.18.hidden_ref = bf16[1,2,8,76,1024]{4,3,2,1,0:T(8,128)(2,1)} copy(bf16[1,2,8,76,1024]{4,2,3,1,0:T(8,128)(2,1)S(1)} %copy-done.1) | data formatting | bytes 4980736 | tf_op args[5]
  49.2 11.3 %project.1 = bf16[8,1280,256]{2,1,0:T(8,128)(2,1)} custom-call(bf16[1,2,8,76,1024]{4,3,2,1,0:T(8,128)(2,1)} %copy.18.hidden_ref, bf16[1,1024,1024]{2,1,0:T(8,128)(2,1)} %wk_ref.1, bf16[1,1024,1024]{2,1,0:T(8,128)(2,1)} %wv_ref.1), custom_call_target="tpu_custom_call" | custom-call | flops 5368709120 | bytes 11927552 | tf_op jit(solution)/shard_map/project/pallas_call | solution.py:157
  60.5 0.0 reduce-scatter.2.cloned.1.call-update
  60.5 125.2 %all-to-all-done.1.rest_0_.rest_1_.rest_2_.rest_3_.rest_4_.rest_5_.rest_6_.rest_7_ = bf16[32,384,256]{2,1,0:T(8,128)(2,1)} async-done(((bf16[32,384,256]{2,1,0:T(8,128)(2,1)}), bf16[32,384,256]{2,1,0:T(8,128)(2,1)}, u32[]{:S(2)}, u32[]{:S(2)}) %all-to-all-start.1) | async-done | bytes 6291488 | tf_op jit(solution)/shard_map/all_to_all | solution.py:388
  185.7 9.0 %all-to-all-start.2 = ((bf16[32,64,256]{2,1,0:T(8,128)(2,1)}), bf16[32,64,256]{2,1,0:T(8,128)(2,1)S(1)}, u32[]{:S(2)}, u32[]{:S(2)}) async-start(bf16[32,64,256]{2,1,0:T(8,128)(2,1)} %get-tuple-element.16), calls=%async_computation.3 | async-start | bytes 2097152 | tf_op jit(solution)/shard_map/all_to_all | solution.py:396
  194.7 0.5 and_select_fusion.place_ref
  195.2 0.0 reduce-scatter.2.cloned.1.call-done.fresh_ref
  195.2 30.2 %attend_main.1 = (f32[2,8,256,256]{3,2,1,0:T(8,128)}, f32[2,8,256,128]{3,2,1,0:T(8,128)}) custom-call(s32[16]{0:T(128)} %and_select_fusion.place_ref, bf16[1,2,256,1024]{3,2,1,0:T(8,128)(2,1)} %q_ref.3, bf16[1280,256]{1,0:T(8,128)(2,1)} %reduce-scatter.2.cloned.1.call-done.fresh_ref, bf16[1,2,256,128]{3,2,1,0:T(8,128)(2,1)} %nk_ref.1, ...), custom_call_target="tpu_custom_call" | custom-call | flops 12482248704 | bytes 10354688 | tf_op jit(solution)/shard_map/attend_main/pallas_call | solution.py:261
  225.5 0.0 all-to-all-done.2.rest_0_.rest_1_.rest_2_.rest_3_.rest_4_.rest_5_.rest_6_.rest_7_
  225.5 0.0 copy-start
  225.5 1.0 copy-done
  226.5 8.6 %attend_last.1 = bf16[1,2,256,1024]{3,2,1,0:T(8,128)(2,1)} custom-call(s32[16]{0:T(128)} %and_select_fusion.place_ref, bf16[1,2,256,1024]{3,2,1,0:T(8,128)(2,1)} %q_ref.3, f32[2,8,256,256]{3,2,1,0:T(8,128)} %get-tuple-element.14.acc_in, f32[2,8,256,128]{3,2,1,0:T(8,128)} %get-tuple-element.15.top_in, bf16[32,64,256]{2,1,0:T(8,128)(2,1)} %copy-done, ...), custom_call_target="tpu_custom_call" | custom-call | flops 1610612736 | bytes 6815744 | tf_op jit(solution)/shard_map/attend_last/pallas_call | solution.py:315
  (2 shorter events, 0.0 us)
Async XLA Ops:
  9.3 22.7 %all-to-all-start = ((s32[16,1,16]{2,1,0:T(1,128)}), s32[16,1,16]{2,1,0:T(1,128)S(1)}, u32[]{:S(2)}, u32[]{:S(2)}) async-start(s32[16,1,16]{2,1,0:T(1,128)} %broadcast_in_dim.26), calls=%async_computation.1 | async-start | bytes 16384 | tf_op jit(solution)/shard_map/all_to_all | solution.py:372
  37.5 8.8 %copy-start.1 = (bf16[1,2,8,76,1024]{4,2,3,1,0:T(8,128)(2,1)S(1)}, bf16[1,2,8,76,1024]{4,2,3,1,0:T(8,128)(2,1)}, u32[]{:S(2)}) copy-start(bf16[1,2,8,76,1024]{4,2,3,1,0:T(8,128)(2,1)} %param.16) | copy-start | bytes 7471108
  37.6 148.2 %all-to-all-start.1 = ((bf16[32,384,256]{2,1,0:T(8,128)(2,1)}), bf16[32,384,256]{2,1,0:T(8,128)(2,1)}, u32[]{:S(2)}, u32[]{:S(2)}) async-start(bf16[32,384,256]{2,1,0:T(8,128)(2,1)} %get-tuple-element.12), calls=%async_computation.2 | async-start | bytes 12582912 | tf_op jit(solution)/shard_map/all_to_all | solution.py:388
  46.3 148.9 %reduce-scatter.2.cloned.1.call-start = ((), (), s32[]{:S(2)}) async-start(), calls=%async_computation.4 | async-start | bytes 5898240 | tf_op jit(solution)/shard_map/reduce_scatter | solution.py:389
  185.7 39.8 %all-to-all-start.2 = ((bf16[32,64,256]{2,1,0:T(8,128)(2,1)}), bf16[32,64,256]{2,1,0:T(8,128)(2,1)S(1)}, u32[]{:S(2)}, u32[]{:S(2)}) async-start(bf16[32,64,256]{2,1,0:T(8,128)(2,1)} %get-tuple-element.16), calls=%async_computation.3 | async-start | bytes 2097152 | tf_op jit(solution)/shard_map/all_to_all | solution.py:396
  225.5 1.0 copy-start
Sparse Core Ops, SparseCore 0:
  60.7 127.4 reduce-scatter.1

commit v2 on v1

v2 whole, which is shorter than its diff:
```python
import functools

import jax
import jax.numpy as jnp
from jax import lax
from jax.experimental import pallas as pl
from jax.experimental.pallas import tpu as pltpu
from jax.sharding import PartitionSpec as P

HD = 128
TILE = 16
MIB = 1 << 20
LOG2E = 1.4426950408889634


def ceil_to(n, m):
    return -(-n // m) * m


def compact_kernel(ids_ref, rows_ref, ck_ref, cv_ref, out_ref, *, kept):
    layers, some, clen, width = ck_ref.shape
    padded = out_ref.shape[2]
    rr = rows_ref.shape[1]
    earlier = (
        lax.broadcasted_iota(jnp.int32, (clen, clen), 0)
        < lax.broadcasted_iota(jnp.int32, (clen, clen), 1)
    ).astype(jnp.bfloat16)
    ones = jnp.ones((8, rr), jnp.bfloat16)
    target = lax.broadcasted_iota(jnp.int32, (padded, clen), 0)
    target = jnp.where(target < kept, target, 0)
    keeps = []
    for i in range(some):
        rows = rows_ref[pl.ds(ids_ref[pl.program_id(0) * some + i], 1), :]
        hit = (lax.broadcasted_iota(jnp.int32, (clen, rr), 0) == rows).astype(jnp.bfloat16)
        gone = lax.dot_general(
            ones, hit, (((1,), (1,)), ((), ())), preferred_element_type=jnp.float32
        )
        keeps.append(1.0 - gone)
    ranks = jnp.dot(
        jnp.concatenate(keeps, axis=0).astype(jnp.bfloat16),
        earlier,
        preferred_element_type=jnp.float32,
    )
    for i in range(some):
        rank = ranks[8 * i : 8 * i + 1].astype(jnp.int32)
        rank = jnp.where(keeps[i][:1] > 0.5, rank, -1)
        pick = (target == rank).astype(jnp.bfloat16)
        for layer in range(layers):
            both = jnp.concatenate([ck_ref[layer, i], cv_ref[layer, i]], axis=1)
            out_ref[layer, i] = jnp.dot(
                pick, both, preferred_element_type=jnp.float32
            ).astype(out_ref.dtype)


def compact(ids, recompute_rows, cache_keys, cache_values, kept, padded):
    layers, spans, clen, width = cache_keys.shape
    some = spans // 2
    cache_spec = pl.BlockSpec((layers, some, clen, width), lambda i, ids: (0, i, 0, 0))
    return pl.pallas_call(
        functools.partial(compact_kernel, kept=kept),
        grid_spec=pltpu.PrefetchScalarGridSpec(
            num_scalar_prefetch=1,
            grid=(spans // some,),
            in_specs=[
                pl.BlockSpec(recompute_rows.shape, lambda i, ids: (0, 0)),
                cache_spec,
                cache_spec,
            ],
            out_specs=pl.BlockSpec(
                (layers, some, padded, 2 * width), lambda i, ids: (0, i, 0, 0)
            ),
        ),
        out_shape=jax.ShapeDtypeStruct((layers, spans, padded, 2 * width), jnp.bfloat16),
        compiler_params=pltpu.CompilerParams(vmem_limit_bytes=56 * MIB),
        cost_estimate=pl.CostEstimate(
            flops=2 * layers * spans * padded * clen * 2 * width,
            bytes_accessed=8 * layers * spans * clen * width,
            transcendentals=0,
        ),
        name="compact",
    )(ids, recompute_rows, cache_keys, cache_values)


def spread_kernel(local_ref, packed_ref, main_ref, rest_ref, sem, *, groups, cut):
    layers, _, padded, _ = packed_ref.shape

    def copies(g):
        made = []
        for layer in range(layers):
            dest = layer * groups + g
            made.append(
                pltpu.make_async_copy(
                    packed_ref.at[layer, local_ref[g], pl.ds(0, cut)],
                    main_ref.at[dest],
                    sem.at[0, dest],
                )
            )
            made.append(
                pltpu.make_async_copy(
                    packed_ref.at[layer, local_ref[g], pl.ds(cut, padded - cut)],
                    rest_ref.at[dest],
                    sem.at[1, dest],
                )
            )
        return made

    for g in range(groups):

        @pl.when(local_ref[g] >= 0)
        def _():
            for copy in copies(g):
                copy.start()

    for g in range(groups):

        @pl.when(local_ref[g] >= 0)
        def _():
            for copy in copies(g):
                copy.wait()


def spread(local, packed, cut):
    layers, spans, padded, wide = packed.shape
    groups = local.shape[0]
    dests = layers * groups
    return pl.pallas_call(
        functools.partial(spread_kernel, groups=groups, cut=cut),
        in_specs=[
            pl.BlockSpec(memory_space=pltpu.SMEM),
            pl.BlockSpec(memory_space=pltpu.VMEM),
        ],
        out_specs=[pl.BlockSpec(memory_space=pl.ANY), pl.BlockSpec(memory_space=pl.ANY)],
        out_shape=[
            jax.ShapeDtypeStruct((dests, cut, wide), jnp.bfloat16),
            jax.ShapeDtypeStruct((dests, padded - cut, wide), jnp.bfloat16),
        ],
        scratch_shapes=[pltpu.SemaphoreType.DMA((2, dests))],
        compiler_params=pltpu.CompilerParams(vmem_limit_bytes=56 * MIB),
        cost_estimate=pl.CostEstimate(
            flops=0, bytes_accessed=2 * (dests + layers * spans) * padded * wide, transcendentals=0
        ),
        name="spread",
    )(local, packed)


def project_kernel(hidden_ref, wk_ref, wv_ref, out_ref, rows_ref, *, rrows, slot):
    _, reqs, topk, _, _ = hidden_ref.shape

    @pl.when(pl.program_id(0) == 0)
    def _():
        for r in range(reqs):
            for j in range(topk):
                at = (r * topk + j) * slot
                rows_ref[at : at + rrows] = hidden_ref[0, r, j]
                if slot > rrows:
                    rows_ref[at + rrows : at + slot] = hidden_ref[0, r, j, : slot - rrows]

    weight = jnp.concatenate([wk_ref[0], wv_ref[0]], axis=1)
    out_ref[0] = jnp.dot(
        rows_ref[...], weight, preferred_element_type=jnp.float32
    ).astype(out_ref.dtype)


def project(hidden, w_key, w_value, slot, parts):
    _, reqs, topk, rrows, feats = hidden.shape
    spans = reqs * topk
    share = w_key.shape[2] // parts
    return pl.pallas_call(
        functools.partial(project_kernel, rrows=rrows, slot=slot),
        grid=(parts,),
        in_specs=[
            pl.BlockSpec(hidden.shape, lambda p: (0, 0, 0, 0, 0)),
            pl.BlockSpec((1, feats, share), lambda p: (0, 0, p)),
            pl.BlockSpec((1, feats, share), lambda p: (0, 0, p)),
        ],
        out_specs=pl.BlockSpec((1, spans * slot, 2 * share), lambda p: (p, 0, 0)),
        out_shape=jax.ShapeDtypeStruct((parts, spans * slot, 2 * share), jnp.bfloat16),
        scratch_shapes=[pltpu.VMEM((spans * slot, feats), jnp.bfloat16)],
        compiler_params=pltpu.CompilerParams(vmem_limit_bytes=56 * MIB),
        cost_estimate=pl.CostEstimate(
            flops=4 * parts * spans * slot * feats * share,
            bytes_accessed=2 * spans * rrows * feats + 4 * parts * (feats + spans * slot) * share,
            transcendentals=0,
        ),
        name="project",
    )(hidden, w_key, w_value)


def attend_head(q, key_ref, wide_ref, state, causal):
    qlen = q.shape[0]
    count = key_ref.shape[0]
    factor = LOG2E / (HD ** 0.5)
    scores = lax.dot_general(
        q, key_ref[...], (((1,), (1,)), ((), ())), preferred_element_type=jnp.float32
    )
    if causal is not None:
        scores = jnp.concatenate(
            [scores[:, : count - qlen], jnp.where(causal, scores[:, count - qlen :], -1e30)],
            axis=1,
        )
    top = jnp.max(scores, axis=1, keepdims=True) * factor
    if state is not None:
        old = state[:, 2 * HD - 1 :]
        top = jnp.maximum(old, top)
    probs = jnp.exp2(scores * factor - top).astype(jnp.bfloat16)
    total = jnp.dot(probs, wide_ref[...], preferred_element_type=jnp.float32)
    if state is not None:
        total = total + state * jnp.exp2(old - top)
    return total, top


def pack_state(total, top):
    lane = lax.broadcasted_iota(jnp.int32, total.shape, 1)
    return jnp.where(lane < 2 * HD - HD // 2, total, top)


def gather_keys(blocks, key_ref, wide_ref, kept):
    rows = blocks[0].shape[1]
    real = lax.broadcasted_iota(jnp.int32, (rows, HD), 0) < kept
    for j, ref in enumerate(blocks):
        span = slice(j * rows, (j + 1) * rows)
        key_ref[span] = ref[0, :, :HD]
        value = ref[0, :, HD:]
        if kept < rows:
            value = jnp.where(real, value, 0).astype(jnp.bfloat16)
        wide_ref[span, :HD] = value
        wide_ref[span, HD:] = real.astype(jnp.bfloat16)


def own_kernel(
    q_ref, half_ref, other_ref, nk_ref, nv_ref, out_ref, key_ref, wide_ref, *, rrows, slot
):
    fresh_rows = half_ref.shape[0]
    qlen = nk_ref.shape[2]

    @pl.when(pl.program_id(1) == 0)
    def _():
        real = lax.broadcasted_iota(jnp.int32, (fresh_rows, HD), 0) % slot < rrows
        fresh = half_ref[...].astype(jnp.float32) + other_ref[...].astype(jnp.float32)
        key_ref[:fresh_rows] = fresh[:, :HD].astype(jnp.bfloat16)
        wide_ref[:fresh_rows, :HD] = jnp.where(real, fresh[:, HD:], 0).astype(jnp.bfloat16)
        wide_ref[:fresh_rows, HD:] = real.astype(jnp.bfloat16)
        key_ref[fresh_rows:] = nk_ref[0, 0]
        wide_ref[fresh_rows:, :HD] = nv_ref[0, 0]
        wide_ref[fresh_rows:, HD:] = jnp.ones((qlen, HD), jnp.bfloat16)

    causal = lax.broadcasted_iota(jnp.int32, (qlen, qlen), 0) >= lax.broadcasted_iota(
        jnp.int32, (qlen, qlen), 1
    )
    for h in range(out_ref.shape[1]):
        q = q_ref[0, 0, :, h * HD : (h + 1) * HD]
        out_ref[0, h] = pack_state(*attend_head(q, key_ref, wide_ref, None, causal))


def main_kernel(place_ref, q_ref, state_ref, *rest):
    out_ref, key_ref, wide_ref = rest[-3:]
    blocks = rest[:-3]

    @pl.when(pl.program_id(1) == 0)
    def _():
        gather_keys(blocks, key_ref, wide_ref, blocks[0].shape[1])

    for h in range(out_ref.shape[1]):
        q = q_ref[0, 0, :, h * HD : (h + 1) * HD]
        out_ref[0, h] = pack_state(*attend_head(q, key_ref, wide_ref, state_ref[0, h], None))


def last_kernel(place_ref, q_ref, state_ref, *rest, kept):
    out_ref, key_ref, wide_ref = rest[-3:]
    blocks = rest[:-3]

    @pl.when(pl.program_id(1) == 0)
    def _():
        gather_keys(blocks, key_ref, wide_ref, kept)

    for h in range(state_ref.shape[1]):
        lanes = slice(h * HD, (h + 1) * HD)
        total, _ = attend_head(
            q_ref[0, 0, :, lanes], key_ref, wide_ref, state_ref[0, h], None
        )
        out_ref[0, 0, :, lanes] = (total[:, :HD] / total[:, HD : HD + 1]).astype(out_ref.dtype)


def attend_cost(reqs, heads, qlen, count):
    return pl.CostEstimate(
        flops=6 * reqs * heads * qlen * count * HD,
        bytes_accessed=4 * reqs * count * HD + 16 * reqs * heads * qlen * HD,
        transcendentals=reqs * heads * qlen * count,
    )


def attend_own(queries, half, other, query_keys, query_values, rrows, slot):
    _, reqs, qlen, feats = queries.shape
    heads = feats // HD
    some = heads // 2
    fresh_rows = half.shape[0] // reqs
    count = fresh_rows + qlen
    return pl.pallas_call(
        functools.partial(own_kernel, rrows=rrows, slot=slot),
        grid=(reqs, heads // some),
        in_specs=[
            pl.BlockSpec((1, 1, qlen, some * HD), lambda r, h: (0, r, 0, h)),
            pl.BlockSpec((fresh_rows, 2 * HD), lambda r, h: (r, 0)),
            pl.BlockSpec((fresh_rows, 2 * HD), lambda r, h: (r, 0)),
            pl.BlockSpec((1, 1, qlen, HD), lambda r, h: (0, r, 0, 0)),
            pl.BlockSpec((1, 1, qlen, HD), lambda r, h: (0, r, 0, 0)),
        ],
        out_specs=pl.BlockSpec((1, some, qlen, 2 * HD), lambda r, h: (r, h, 0, 0)),
        out_shape=jax.ShapeDtypeStruct((reqs, heads, qlen, 2 * HD), jnp.float32),
        scratch_shapes=[
            pltpu.VMEM((count, HD), jnp.bfloat16),
            pltpu.VMEM((count, 2 * HD), jnp.bfloat16),
        ],
        compiler_params=pltpu.CompilerParams(vmem_limit_bytes=56 * MIB),
        cost_estimate=attend_cost(reqs, heads, qlen, count),
        name="attend_own",
    )(queries, half, other, query_keys, query_values)


def attend_spans(place, queries, state, arrived, kept, last):
    _, reqs, qlen, feats = queries.shape
    heads = feats // HD
    some = heads
    rows = arrived.shape[1]
    topk = place.shape[0] // reqs
    count = topk * rows
    q_spec = pl.BlockSpec((1, 1, qlen, some * HD), lambda r, h, at: (0, r, 0, h))
    state_spec = pl.BlockSpec((1, some, qlen, 2 * HD), lambda r, h, at: (r, h, 0, 0))
    blocks = [
        pl.BlockSpec((1, rows, 2 * HD), lambda r, h, at, j=j: (at[r * topk + j], 0, 0))
        for j in range(topk)
    ]
    return pl.pallas_call(
        functools.partial(last_kernel, kept=kept) if last else main_kernel,
        grid_spec=pltpu.PrefetchScalarGridSpec(
            num_scalar_prefetch=1,
            grid=(reqs, heads // some),
            in_specs=[q_spec, state_spec] + blocks,
            out_specs=q_spec if last else state_spec,
            scratch_shapes=[
                pltpu.VMEM((count, HD), jnp.bfloat16),
                pltpu.VMEM((count, 2 * HD), jnp.bfloat16),
            ],
        ),
        out_shape=jax.ShapeDtypeStruct(queries.shape, jnp.bfloat16)
        if last
        else jax.ShapeDtypeStruct(state.shape, state.dtype),
        compiler_params=pltpu.CompilerParams(vmem_limit_bytes=56 * MIB),
        cost_estimate=attend_cost(reqs, heads, qlen, count),
        name="attend_last" if last else "attend_main",
    )(place, queries, state, *([arrived] * topk))


def on_device(
    cache_keys,
    cache_values,
    span_ids,
    owner_slot,
    recompute_rows,
    hidden,
    w_key,
    w_value,
    queries,
    query_keys,
    query_values,
):
    sections = lax.axis_size("section")
    groups = lax.axis_size("dp")
    parts = lax.axis_size("tensor")
    per_owner = cache_keys.shape[1]
    clen = cache_keys.shape[2]
    req_dev, topk = span_ids.shape
    rrows = hidden.shape[3]
    kept = clen - rrows
    cut = kept // HD * HD
    padded = ceil_to(kept, 64)
    slot = ceil_to(rrows, TILE)
    myself = lax.axis_index("section") * groups + lax.axis_index("dp")

    own_slot = owner_slot[span_ids].reshape(req_dev * topk)
    every_slot = lax.all_to_all(
        jnp.broadcast_to(own_slot[None], (groups, req_dev * topk)), "dp", 0, 0
    )

    here = myself * per_owner + jnp.arange(per_owner, dtype=jnp.int32)
    held = owner_slot[None, :] == here[:, None]
    ids = jnp.sum(
        jnp.where(held, jnp.arange(owner_slot.shape[0], dtype=jnp.int32)[None], 0), axis=1
    )
    packed = compact(ids, recompute_rows, cache_keys, cache_values, kept, padded)

    mine = every_slot // per_owner == myself
    local = jnp.max(jnp.where(mine, every_slot % per_owner, -1), axis=1)
    main, rest = spread(local, packed, cut)
    main, hidden = lax.optimization_barrier((main, hidden))
    partial = project(hidden, w_key, w_value, slot, parts)
    arrived = lax.all_to_all(main, ("section", "dp"), 0, 0, tiled=True)
    outer = parts // 2
    along_y = [[2 * y + x for y in range(outer)] for x in range(2)]
    fresh = lax.psum_scatter(
        partial.reshape(parts * req_dev * topk * slot, -1),
        "tensor",
        scatter_dimension=0,
        tiled=True,
        axis_index_groups=along_y,
    ).reshape(2, req_dev * topk * slot, -1)
    side = lax.axis_index("tensor") % 2
    mine_half = lax.dynamic_index_in_dim(fresh, side, 0, keepdims=False)
    their_half = lax.dynamic_index_in_dim(fresh, 1 - side, 0, keepdims=False)
    other_half = lax.ppermute(their_half, "tensor", [(i, i ^ 1) for i in range(parts)])
    state = attend_own(
        queries, mine_half, other_half, query_keys, query_values, rrows, slot
    )
    rest, arrived, state = lax.optimization_barrier((rest, arrived, state))
    arrived_rest = lax.all_to_all(rest, ("section", "dp"), 0, 0, tiled=True)

    place = own_slot // per_owner
    state = attend_spans(place, queries, state, arrived, cut, False)
    return attend_spans(place, queries, state, arrived_rest, kept - cut, True)


def solution(mesh):
    in_specs = (
        P(None, ("section", "dp"), None, "tensor"),
        P(None, ("section", "dp"), None, "tensor"),
        P("dp", None),
        P(),
        P(),
        P("section", "dp", None, None, "tensor"),
        P("section", "tensor", None),
        P("section", "tensor", None),
        P("section", "dp", None, "tensor"),
        P("section", "dp", None, "tensor"),
        P("section", "dp", None, "tensor"),
    )
    out_specs = P("section", "dp", None, "tensor")
    return jax.shard_map(
        on_device, mesh=mesh, in_specs=in_specs, out_specs=out_specs, check_vma=False
    )
```

time: 242 us -> 235 us (0.971)
  waiting for transfers between devices: 125 us -> 115 us
  local copies, waits for them, and re-layouts: 7.47 us -> 10.6 us
    all_to_all x1, waiting for transfers between devices: 125 us -> 26.6 us  [on_device(): arrived = lax.all_to_all(main, ('section', 'dp'), 0, 0, tiled=True)]
    reduce_scatter x1, waiting for transfers between devices: 0.01 us -> 59.1 us  [on_device(): lax.psum_scatter(partial.reshape(parts * req_dev * topk * slot, -1), 'ten...]
    ppermute x0 -> x1, waiting for transfers between devices: none -> 24 us  [on_device(): lax.ppermute(their_half, 'tensor', [(i, i ^ 1) for i in range(parts)])]
    all_to_all x1, waiting for transfers between devices: 0.01 us -> 4.77 us  [on_device(): arrived_rest = lax.all_to_all(rest, ('section', 'dp'), 0, 0, tiled=True)]
    pallas_call x1, Pallas kernels: 9.74 us -> 6.44 us  [compact(): pl.pallas_call(functools.partial(compact_kernel, kept=kept), grid_spec=pl...]
    optimization_barrier x0 -> x1, local copies, waits for them, and re-layouts: none -> 2.85 us  [on_device(): main, hidden = lax.optimization_barrier((main, hidden))]
    ppermute x0 -> x1, starting transfers between devices: none -> 2.72 us  [on_device(): lax.ppermute(their_half, 'tensor', [(i, i ^ 1) for i in range(parts)])]
    unnamed x6 -> x7, local copies, waits for them, and re-layouts: 5.45 us -> 3.47 us
  transfers between devices with their start and end apart: 4 -> 5, of which waited for: 1 -> 4; matrix products, arithmetic and copies ran while one was open for 3% -> 4% of each run, Pallas kernels for 21% -> 21%
where the time goes in v2:
time: 235 us; the launch traced here: 234 us
  waiting for transfers between devices  115 us (49%)
  Pallas kernels  62.3 us (27%)
  starting transfers between devices  29.5 us (13%)
  between operations  13.5 us (6%)
  local copies, waits for them, and re-layouts  10.6 us (5%)
  other arithmetic  3.27 us (1%)
    reduce_scatter x1, waiting for transfers between devices, on_device(): lax.psum_scatter(partial.reshape(parts * req_dev * topk * slot, -1), 'ten...  59.1 us
    pallas_call x2, Pallas kernels, attend_spans(): pl.pallas_call(functools.partial(last_kernel, kept=kept) if last else mai...  29.7 us
    all_to_all x1, waiting for transfers between devices, on_device(): arrived = lax.all_to_all(main, ('section', 'dp'), 0, 0, tiled=True)  26.6 us
    ppermute x1, waiting for transfers between devices, on_device(): lax.ppermute(their_half, 'tensor', [(i, i ^ 1) for i in range(parts)])  24 us
    pallas_call x1, Pallas kernels, project(): pl.pallas_call(functools.partial(project_kernel, rrows=rrows, slot=slot),...  11.3 us
    all_to_all x1, starting transfers between devices, on_device(): lax.all_to_all(jnp.broadcast_to(own_slot[None], (groups, req_dev * topk))...  9.98 us
    pallas_call x1, Pallas kernels, attend_own(): pl.pallas_call(functools.partial(own_kernel, rrows=rrows, slot=slot), gri...  9.57 us
    all_to_all x1, starting transfers between devices, on_device(): arrived_rest = lax.all_to_all(rest, ('section', 'dp'), 0, 0, tiled=True)  8.95 us
  transfers between devices with their start and end apart: 5, of which 4 were waited for; matrix products, arithmetic and copies ran while one was open for 4% of the time, Pallas kernels for 21%

profile of v2, /device:TPU:1, one launch (start us, length us, event | category | flops | bytes accessed | tf_op | source)
XLA Modules:
  0.0 233.6 jit_solution(15106359350479420110)
XLA Ops:
  6.5 0.7 compare_select_fusion
  7.2 0.1 reshape.27
  7.3 1.3 gather_fusion
  8.7 0.6 broadcast_in_dim.26
  9.3 10.0 %all-to-all-start = ((s32[16,1,16]{2,1,0:T(1,128)}), s32[16,1,16]{2,1,0:T(1,128)S(1)}, u32[]{:S(2)}, u32[]{:S(2)}) async-start(s32[16,1,16]{2,1,0:T(1,128)} %broadcast_in_dim.26), calls=%async_computation | async-start | bytes 16384 | tf_op jit(solution)/shard_map/all_to_all | solution.py:381
  19.2 1.4 select_reduce_fusion.ids_ref
  20.7 1.6 copy.18.rows_ref
  22.3 6.4 %compact.1.packed_ref = bf16[2,8,448,256]{3,2,1,0:T(8,128)(2,1)} custom-call(s32[8]{0:T(128)} %select_reduce_fusion.ids_ref, s32[256,76]{1,0:T(8,128)} %copy.18.rows_ref, bf16[2,8,512,128]{3,2,1,0:T(8,128)(2,1)} %ck_ref.1, bf16[2,8,512,128]{3,2,1,0:T(8,128)(2,1)} %cv_ref.1), custom_call_target="tpu_custom_call" | custom-call | flops 1879048192 | bytes 8388608 | tf_op jit(solution)/shard_map/compact/pallas_call | solution.py:59
  28.8 0.0 all-to-all-done
  28.8 0.6 fusion.2.local_ref
  29.4 5.3 %spread.1 = (bf16[32,384,256]{2,1,0:T(8,128)(2,1)}, bf16[32,64,256]{2,1,0:T(8,128)(2,1)}) custom-call(s32[16]{0:T(128)} %fusion.2.local_ref, bf16[2,8,448,256]{3,2,1,0:T(8,128)(2,1)} %compact.1.packed_ref), custom_call_target="tpu_custom_call" | custom-call | bytes 11010048 | tf_op jit(solution)/shard_map/spread/pallas_call | solution.py:126
  34.7 0.0 copy-start.1
  34.7 7.8 %all-to-all-start.1 = ((bf16[32,384,256]{2,1,0:T(8,128)(2,1)}), bf16[32,384,256]{2,1,0:T(8,128)(2,1)}, u32[]{:S(2)}, u32[]{:S(2)}) async-start(bf16[32,384,256]{2,1,0:T(8,128)(2,1)} %get-tuple-element.14), calls=%async_computation.1 | async-start | bytes 12582912 | tf_op jit(solution)/shard_map/all_to_all | solution.py:397
  42.5 0.0 reduce-scatter.2.cloned.1.call-start
  42.6 0.0 copy-done.1
  42.6 2.8 %copy.19.hidden_ref = bf16[1,2,8,76,1024]{4,3,2,1,0:T(8,128)(2,1)} copy(bf16[1,2,8,76,1024]{4,2,3,1,0:T(8,128)(2,1)S(1)} %copy-done.1) | data formatting | bytes 4980736 | tf_op jit(solution)/shard_map/optimization_barrier | solution.py:395
  45.5 11.3 %project.1 = bf16[8,1280,256]{2,1,0:T(8,128)(2,1)} custom-call(bf16[1,2,8,76,1024]{4,3,2,1,0:T(8,128)(2,1)} %copy.19.hidden_ref, bf16[1,1024,1024]{2,1,0:T(8,128)(2,1)} %wk_ref.1, bf16[1,1024,1024]{2,1,0:T(8,128)(2,1)} %wv_ref.1), custom_call_target="tpu_custom_call" | custom-call | flops 5368709120 | bytes 11927552 | tf_op jit(solution)/shard_map/project/pallas_call | solution.py:168
  56.7 0.0 reduce-scatter.2.cloned.1.call-update
  56.8 59.1 %reduce-scatter.2.cloned.1.call-done = bf16[2560,256]{1,0:T(8,128)(2,1)} async-done(((bf16[10240,256]{1,0:T(8,128)(2,1)}), bf16[2560,256]{1,0:T(8,128)(2,1)}) %reduce-scatter.2.cloned.1.call-update) | async-done | bytes 1310736 | tf_op jit(solution)/shard_map/reduce_scatter | solution.py:400
  115.9 2.2 dynamic-slice_bitcast_fusion
  118.1 2.7 %collective-permute-start = (bf16[1280,256]{1,0:T(8,128)(2,1)S(1)}, bf16[1280,256]{1,0:T(8,128)(2,1)S(1)}, u32[]{:S(2)}, u32[]{:S(2)}) collective-permute-start(bf16[1280,256]{1,0:T(8,128)(2,1)S(1)} %get-tuple-element.19), channel_id=1, source_target_pairs={{0,1},{1,0},{2,3},{3,2},{4,5},{5,4},{6,7},{7,6},{8,9},{9,8},{10,11... | collective-permute-start | bytes 1966088 | tf_op jit(solution)/shard_map/ppermute | solution.py:410
  120.8 24.0 %collective-permute-done.other_ref = bf16[1280,256]{1,0:T(8,128)(2,1)S(1)} collective-permute-done((bf16[1280,256]{1,0:T(8,128)(2,1)S(1)}, bf16[1280,256]{1,0:T(8,128)(2,1)S(1)}, u32[]{:S(2)}, u32[]{:S(2)}) %collective-permute-start) | collective-permute-done | bytes 655392 | tf_op jit(solution)/shard_map/ppermute | solution.py:410
  144.8 0.0 copy-start.2
  144.8 0.9 copy-done.2
  145.7 9.6 %attend_own.1.state_ref = f32[2,8,256,256]{3,2,1,0:T(8,128)} custom-call(bf16[1,2,256,1024]{3,2,1,0:T(8,128)(2,1)} %q_ref.5, bf16[1280,256]{1,0:T(8,128)(2,1)} %get-tuple-element.20.half_ref, bf16[1280,256]{1,0:T(8,128)(2,1)} %copy-done.2, bf16[1,2,256,128]{3,2,1,0:T(8,128)(2,1)} %nk_ref.1, bf16[1,2,256,128]{3,2,1,0:T(8,128)(2,1)} %nv_ref.1), custom_call_target="tpu_custom_call" | custom-call | flops 2818572288 | bytes 9306112 | tf_op jit(solution)/shard_map/attend_own/pallas_call | solution.py:298
  155.2 26.6 %all-to-all-done.1.rest_0_.rest_1_.rest_2_.rest_3_.rest_4_.rest_5_.rest_6_.rest_7_ = bf16[32,384,256]{2,1,0:T(8,128)(2,1)} async-done(((bf16[32,384,256]{2,1,0:T(8,128)(2,1)}), bf16[32,384,256]{2,1,0:T(8,128)(2,1)}, u32[]{:S(2)}, u32[]{:S(2)}) %all-to-all-start.1) | async-done | bytes 6291488 | tf_op jit(solution)/shard_map/all_to_all | solution.py:397
  181.9 9.0 %all-to-all-start.2 = ((bf16[32,64,256]{2,1,0:T(8,128)(2,1)}), bf16[32,64,256]{2,1,0:T(8,128)(2,1)S(1)}, u32[]{:S(2)}, u32[]{:S(2)}) async-start(bf16[32,64,256]{2,1,0:T(8,128)(2,1)} %get-tuple-element.18), calls=%async_computation.3 | async-start | bytes 2097152 | tf_op jit(solution)/shard_map/all_to_all | solution.py:415
  190.8 0.5 and_select_fusion.place_ref
  191.4 21.1 %attend_main.1.state_ref = f32[2,8,256,256]{3,2,1,0:T(8,128)} custom-call(s32[16]{0:T(128)} %and_select_fusion.place_ref, bf16[1,2,256,1024]{3,2,1,0:T(8,128)(2,1)} %q_ref.5, f32[2,8,256,256]{3,2,1,0:T(8,128)} %attend_own.1.state_ref, bf16[32,384,256]{2,1,0:T(8,128)(2,1)} %all-to-all-done.1.rest_0_.rest_1_.rest_2_.rest_3_.rest_4_.rest_5_.rest_6_.rest_7_, ...), custom_call_target="tpu_custom_call" | custom-call | flops 9663676416 | bytes 11534336 | tf_op jit(solution)/shard_map/attend_main/pallas_call | solution.py:333
  212.5 4.8 %all-to-all-done.2.rest_0_.rest_1_.rest_2_.rest_3_.rest_4_.rest_5_.rest_6_.rest_7_ = bf16[32,64,256]{2,1,0:T(8,128)(2,1)S(1)} async-done(((bf16[32,64,256]{2,1,0:T(8,128)(2,1)}), bf16[32,64,256]{2,1,0:T(8,128)(2,1)S(1)}, u32[]{:S(2)}, u32[]{:S(2)}) %all-to-all-start.2) | async-done | bytes 1048608 | tf_op jit(solution)/shard_map/all_to_all | solution.py:415
  217.3 1.0 copy-done
  218.2 8.5 %attend_last.1 = bf16[1,2,256,1024]{3,2,1,0:T(8,128)(2,1)} custom-call(s32[16]{0:T(128)} %and_select_fusion.place_ref, bf16[1,2,256,1024]{3,2,1,0:T(8,128)(2,1)} %q_ref.5, f32[2,8,256,256]{3,2,1,0:T(8,128)} %attend_main.1.state_ref, bf16[32,64,256]{2,1,0:T(8,128)(2,1)} %copy-done, bf16[32,64,256]{2,1,0:T(8,128)(2,1)} %copy-done, ...), custom_call_target="tpu_custom_call" | custom-call | flops 1610612736 | bytes 8912896 | tf_op jit(solution)/shard_map/attend_last/pallas_call | solution.py:333
  (3 shorter events, 0.0 us)
Async XLA Ops:
  9.3 19.5 %all-to-all-start = ((s32[16,1,16]{2,1,0:T(1,128)}), s32[16,1,16]{2,1,0:T(1,128)S(1)}, u32[]{:S(2)}, u32[]{:S(2)}) async-start(s32[16,1,16]{2,1,0:T(1,128)} %broadcast_in_dim.26), calls=%async_computation | async-start | bytes 16384 | tf_op jit(solution)/shard_map/all_to_all | solution.py:381
  34.7 7.9 %copy-start.1 = (bf16[1,2,8,76,1024]{4,2,3,1,0:T(8,128)(2,1)S(1)}, bf16[1,2,8,76,1024]{4,2,3,1,0:T(8,128)(2,1)}, u32[]{:S(2)}) copy-start(bf16[1,2,8,76,1024]{4,2,3,1,0:T(8,128)(2,1)} %param.16) | copy-start | bytes 7471108
  34.7 147.2 %all-to-all-start.1 = ((bf16[32,384,256]{2,1,0:T(8,128)(2,1)}), bf16[32,384,256]{2,1,0:T(8,128)(2,1)}, u32[]{:S(2)}, u32[]{:S(2)}) async-start(bf16[32,384,256]{2,1,0:T(8,128)(2,1)} %get-tuple-element.14), calls=%async_computation.1 | async-start | bytes 12582912 | tf_op jit(solution)/shard_map/all_to_all | solution.py:397
  42.5 73.3 %reduce-scatter.2.cloned.1.call-start = ((), (), s32[]{:S(2)}) async-start(), calls=%async_computation.4 | async-start | bytes 6553600 | tf_op jit(solution)/shard_map/reduce_scatter | solution.py:400
  118.1 26.7 %collective-permute-start = (bf16[1280,256]{1,0:T(8,128)(2,1)S(1)}, bf16[1280,256]{1,0:T(8,128)(2,1)S(1)}, u32[]{:S(2)}, u32[]{:S(2)}) collective-permute-start(bf16[1280,256]{1,0:T(8,128)(2,1)S(1)} %get-tuple-element.19), channel_id=1, source_target_pairs={{0,1},{1,0},{2,3},{3,2},{4,5},{5,4},{6,7},{7,6},{8,9},{9,8},{10,11... | collective-permute-start | bytes 1966088 | tf_op jit(solution)/shard_map/ppermute | solution.py:410
  144.8 0.9 copy-start.2
  181.9 35.4 %all-to-all-start.2 = ((bf16[32,64,256]{2,1,0:T(8,128)(2,1)}), bf16[32,64,256]{2,1,0:T(8,128)(2,1)S(1)}, u32[]{:S(2)}, u32[]{:S(2)}) async-start(bf16[32,64,256]{2,1,0:T(8,128)(2,1)} %get-tuple-element.18), calls=%async_computation.3 | async-start | bytes 2097152 | tf_op jit(solution)/shard_map/all_to_all | solution.py:415
  217.3 1.0 copy-start
Sparse Core Ops, SparseCore 0:
  56.9 58.9 reduce-scatter.1

commit v3 on v2

--- a/solution.py
+++ b/solution.py
@@ -143,10 +143,12 @@
     )(local, packed)
 
 
-def project_kernel(hidden_ref, wk_ref, wv_ref, out_ref, rows_ref, *, rrows, slot):
+def project_kernel(dest_ref, hidden_ref, wk_ref, wv_ref, *rest, rrows, slot):
+    out_refs, rows_ref, result_ref = rest[:-2], rest[-2], rest[-1]
     _, reqs, topk, _, _ = hidden_ref.shape
-
-    @pl.when(pl.program_id(0) == 0)
+    step = pl.program_id(0)
+
+    @pl.when(step == 0)
     def _():
         for r in range(reqs):
             for j in range(topk):
@@ -156,26 +158,39 @@
                     rows_ref[at + rrows : at + slot] = hidden_ref[0, r, j, : slot - rrows]
 
     weight = jnp.concatenate([wk_ref[0], wv_ref[0]], axis=1)
-    out_ref[0] = jnp.dot(
+    result_ref[...] = jnp.dot(
         rows_ref[...], weight, preferred_element_type=jnp.float32
-    ).astype(out_ref.dtype)
-
-
-def project(hidden, w_key, w_value, slot, parts):
+    ).astype(result_ref.dtype)
+    for k, out_ref in enumerate(out_refs):
+
+        @pl.when(step == k)
+        def _():
+            out_ref[...] = result_ref[...]
+
+
+def project(dests, hidden, w_key, w_value, slot):
     _, reqs, topk, rrows, feats = hidden.shape
     spans = reqs * topk
+    parts = dests.shape[0]
     share = w_key.shape[2] // parts
+    shape = (spans * slot, 2 * share)
     return pl.pallas_call(
         functools.partial(project_kernel, rrows=rrows, slot=slot),
-        grid=(parts,),
-        in_specs=[
-            pl.BlockSpec(hidden.shape, lambda p: (0, 0, 0, 0, 0)),
-            pl.BlockSpec((1, feats, share), lambda p: (0, 0, p)),
-            pl.BlockSpec((1, feats, share), lambda p: (0, 0, p)),
-        ],
-        out_specs=pl.BlockSpec((1, spans * slot, 2 * share), lambda p: (p, 0, 0)),
-        out_shape=jax.ShapeDtypeStruct((parts, spans * slot, 2 * share), jnp.bfloat16),
-        scratch_shapes=[pltpu.VMEM((spans * slot, feats), jnp.bfloat16)],
+        grid_spec=pltpu.PrefetchScalarGridSpec(
+            num_scalar_prefetch=1,
+            grid=(parts,),
+            in_specs=[
+                pl.BlockSpec(hidden.shape, lambda p, to: (0, 0, 0, 0, 0)),
+                pl.BlockSpec((1, feats, share), lambda p, to: (0, 0, to[p])),
+                pl.BlockSpec((1, feats, share), lambda p, to: (0, 0, to[p])),
+            ],
+            out_specs=[pl.BlockSpec(shape, lambda p, to: (0, 0))] * parts,
+            scratch_shapes=[
+                pltpu.VMEM((spans * slot, feats), jnp.bfloat16),
+                pltpu.VMEM(shape, jnp.bfloat16),
+            ],
+        ),
+        out_shape=[jax.ShapeDtypeStruct(shape, jnp.bfloat16)] * parts,
         compiler_params=pltpu.CompilerParams(vmem_limit_bytes=56 * MIB),
         cost_estimate=pl.CostEstimate(
             flops=4 * parts * spans * slot * feats * share,
@@ -183,7 +198,7 @@
             transcendentals=0,
         ),
         name="project",
-    )(hidden, w_key, w_value)
+    )(dests, hidden, w_key, w_value)
 
 
 def attend_head(q, key_ref, wide_ref, state, causal):
@@ -227,16 +242,18 @@
         wide_ref[span, HD:] = real.astype(jnp.bfloat16)
 
 
-def own_kernel(
-    q_ref, half_ref, other_ref, nk_ref, nv_ref, out_ref, key_ref, wide_ref, *, rrows, slot
-):
-    fresh_rows = half_ref.shape[0]
+def own_kernel(q_ref, nk_ref, nv_ref, *rest, rrows, slot):
+    out_ref, key_ref, wide_ref = rest[-3:]
+    pieces = rest[:-3]
+    fresh_rows = pieces[0].shape[0]
     qlen = nk_ref.shape[2]
 
     @pl.when(pl.program_id(1) == 0)
     def _():
         real = lax.broadcasted_iota(jnp.int32, (fresh_rows, HD), 0) % slot < rrows
-        fresh = half_ref[...].astype(jnp.float32) + other_ref[...].astype(jnp.float32)
+        fresh = pieces[0][...].astype(jnp.float32)
+        for piece in pieces[1:]:
+            fresh = fresh + piece[...].astype(jnp.float32)
         key_ref[:fresh_rows] = fresh[:, :HD].astype(jnp.bfloat16)
         wide_ref[:fresh_rows, :HD] = jnp.where(real, fresh[:, HD:], 0).astype(jnp.bfloat16)
         wide_ref[:fresh_rows, HD:] = real.astype(jnp.bfloat16)
@@ -289,22 +306,21 @@
     )
 
 
-def attend_own(queries, half, other, query_keys, query_values, rrows, slot):
+def attend_own(queries, pieces, query_keys, query_values, rrows, slot):
     _, reqs, qlen, feats = queries.shape
     heads = feats // HD
     some = heads // 2
-    fresh_rows = half.shape[0] // reqs
+    fresh_rows = pieces[0].shape[0] // reqs
     count = fresh_rows + qlen
     return pl.pallas_call(
         functools.partial(own_kernel, rrows=rrows, slot=slot),
         grid=(reqs, heads // some),
         in_specs=[
             pl.BlockSpec((1, 1, qlen, some * HD), lambda r, h: (0, r, 0, h)),
-            pl.BlockSpec((fresh_rows, 2 * HD), lambda r, h: (r, 0)),
-            pl.BlockSpec((fresh_rows, 2 * HD), lambda r, h: (r, 0)),
             pl.BlockSpec((1, 1, qlen, HD), lambda r, h: (0, r, 0, 0)),
             pl.BlockSpec((1, 1, qlen, HD), lambda r, h: (0, r, 0, 0)),
-        ],
+        ]
+        + [pl.BlockSpec((fresh_rows, 2 * HD), lambda r, h: (r, 0))] * len(pieces),
         out_specs=pl.BlockSpec((1, some, qlen, 2 * HD), lambda r, h: (r, h, 0, 0)),
         out_shape=jax.ShapeDtypeStruct((reqs, heads, qlen, 2 * HD), jnp.float32),
         scratch_shapes=[
@@ -314,7 +330,7 @@
         compiler_params=pltpu.CompilerParams(vmem_limit_bytes=56 * MIB),
         cost_estimate=attend_cost(reqs, heads, qlen, count),
         name="attend_own",
-    )(queries, half, other, query_keys, query_values)
+    )(queries, query_keys, query_values, *pieces)
 
 
 def attend_spans(place, queries, state, arrived, kept, last):
@@ -393,24 +409,20 @@
     local = jnp.max(jnp.where(mine, every_slot % per_owner, -1), axis=1)
     main, rest = spread(local, packed, cut)
     main, hidden = lax.optimization_barrier((main, hidden))
-    partial = project(hidden, w_key, w_value, slot, parts)
+    moves = [(i // 2, i % 2) for i in range(parts)]
+
+    def moved(index, move):
+        return (index // 2 + move[0]) % (parts // 2) * 2 + (index + move[1]) % 2
+
+    me = lax.axis_index("tensor")
+    dests = jnp.stack([moved(me, move) for move in moves]).astype(jnp.int32)
+    partial = project(dests, hidden, w_key, w_value, slot)
     arrived = lax.all_to_all(main, ("section", "dp"), 0, 0, tiled=True)
-    outer = parts // 2
-    along_y = [[2 * y + x for y in range(outer)] for x in range(2)]
-    fresh = lax.psum_scatter(
-        partial.reshape(parts * req_dev * topk * slot, -1),
-        "tensor",
-        scatter_dimension=0,
-        tiled=True,
-        axis_index_groups=along_y,
-    ).reshape(2, req_dev * topk * slot, -1)
-    side = lax.axis_index("tensor") % 2
-    mine_half = lax.dynamic_index_in_dim(fresh, side, 0, keepdims=False)
-    their_half = lax.dynamic_index_in_dim(fresh, 1 - side, 0, keepdims=False)
-    other_half = lax.ppermute(their_half, "tensor", [(i, i ^ 1) for i in range(parts)])
-    state = attend_own(
-        queries, mine_half, other_half, query_keys, query_values, rrows, slot
-    )
+    pieces = [partial[0]] + [
+        lax.ppermute(piece, "tensor", [(i, moved(i, move)) for i in range(parts)])
+        for piece, move in zip(partial[1:], moves[1:])
+    ]
+    state = attend_own(queries, pieces, query_keys, query_values, rrows, slot)
     rest, arrived, state = lax.optimization_barrier((rest, arrived, state))
     arrived_rest = lax.all_to_all(rest, ("section", "dp"), 0, 0, tiled=True)
 

time: 235 us -> 228 us (0.970)
  starting transfers between devices: 29.5 us -> 49 us
  waiting for transfers between devices: 115 us -> 101 us
  between operations: 13.5 us -> 0.18 us
    ppermute x1 -> x7, waiting for transfers between devices: 24 us -> 96.1 us  [on_device(): lax.ppermute(piece, 'tensor', [(i, moved(i, move)) for i in range(parts)])]
    reduce_scatter x1 -> x0, waiting for transfers between devices: 59.1 us -> none  [on_device(): lax.psum_scatter(partial.reshape(parts * req_dev * topk * slot, -1), 'ten...]
    all_to_all x1, waiting for transfers between devices: 26.6 us -> 0.2 us  [on_device(): arrived = lax.all_to_all(main, ('section', 'dp'), 0, 0, tiled=True)]
    ppermute x1 -> x7, starting transfers between devices: 2.72 us -> 14.5 us  [on_device(): lax.ppermute(piece, 'tensor', [(i, moved(i, move)) for i in range(parts)])]
    all_to_all x1, starting transfers between devices: 8.95 us -> 14.9 us  [on_device(): arrived_rest = lax.all_to_all(rest, ('section', 'dp'), 0, 0, tiled=True)]
  transfers between devices with their start and end apart: 5 -> 10, of which waited for: 4 -> 6; matrix products, arithmetic and copies ran while one was open for 4% -> 3% of each run, Pallas kernels for 21% -> 23%
where the time goes in v3:
time: 228 us; the launch traced here: 226 us
  waiting for transfers between devices  101 us (44%)
  Pallas kernels  64 us (28%)
  starting transfers between devices  49 us (21%)
  local copies, waits for them, and re-layouts  8.96 us (4%)
  other arithmetic  3.31 us (1%)
    ppermute x7, waiting for transfers between devices, on_device(): lax.ppermute(piece, 'tensor', [(i, moved(i, move)) for i in range(parts)])  96.1 us
    pallas_call x2, Pallas kernels, attend_spans(): pl.pallas_call(functools.partial(last_kernel, kept=kept) if last else mai...  29.7 us
    all_to_all x1, starting transfers between devices, on_device(): arrived_rest = lax.all_to_all(rest, ('section', 'dp'), 0, 0, tiled=True)  14.9 us
    ppermute x7, starting transfers between devices, on_device(): lax.ppermute(piece, 'tensor', [(i, moved(i, move)) for i in range(parts)])  14.5 us
    pallas_call x1, Pallas kernels, project(): pl.pallas_call(functools.partial(project_kernel, rrows=rrows, slot=slot),...  13 us
    pallas_call x1, Pallas kernels, attend_own(): pl.pallas_call(functools.partial(own_kernel, rrows=rrows, slot=slot), gri...  11.1 us
    all_to_all x1, starting transfers between devices, on_device(): lax.all_to_all(jnp.broadcast_to(own_slot[None], (groups, req_dev * topk))...  9.98 us
    all_to_all x1, starting transfers between devices, on_device(): arrived = lax.all_to_all(main, ('section', 'dp'), 0, 0, tiled=True)  9.67 us
  transfers between devices with their start and end apart: 10, of which 6 were waited for; matrix products, arithmetic and copies ran while one was open for 3% of the time, Pallas kernels for 23%

profile of v3, /device:TPU:1, one launch (start us, length us, event | category | flops | bytes accessed | tf_op | source)
XLA Modules:
  0.0 226.4 jit_solution(17147986910828681822)
XLA Ops:
  0.0 0.7 compare_select_fusion
  0.8 1.3 gather_fusion
  2.1 0.6 broadcast_in_dim.26
  2.7 10.0 %all-to-all-start = ((s32[16,1,16]{2,1,0:T(1,128)}), s32[16,1,16]{2,1,0:T(1,128)S(1)}, u32[]{:S(2)}, u32[]{:S(2)}) async-start(s32[16,1,16]{2,1,0:T(1,128)} %broadcast_in_dim.26), calls=%async_computation | async-start | bytes 16384 | tf_op jit(solution)/shard_map/all_to_all | solution.py:397
  12.7 1.4 select_reduce_fusion.ids_ref
  14.1 1.6 copy.18.rows_ref
  15.7 6.4 %compact.1.packed_ref = bf16[2,8,448,256]{3,2,1,0:T(8,128)(2,1)} custom-call(s32[8]{0:T(128)} %select_reduce_fusion.ids_ref, s32[256,76]{1,0:T(8,128)} %copy.18.rows_ref, bf16[2,8,512,128]{3,2,1,0:T(8,128)(2,1)} %ck_ref.1, bf16[2,8,512,128]{3,2,1,0:T(8,128)(2,1)} %cv_ref.1), custom_call_target="tpu_custom_call" | custom-call | flops 1879048192 | bytes 8388608 | tf_op jit(solution)/shard_map/compact/pallas_call | solution.py:59
  22.2 0.7 fusion.2.local_ref
  22.8 3.7 %spread.1 = (bf16[32,384,256]{2,1,0:T(8,128)(2,1)}, bf16[32,64,256]{2,1,0:T(8,128)(2,1)}) custom-call(s32[16]{0:T(128)} %fusion.2.local_ref, bf16[2,8,448,256]{3,2,1,0:T(8,128)(2,1)} %compact.1.packed_ref), custom_call_target="tpu_custom_call" | custom-call | bytes 11010048 | tf_op jit(solution)/shard_map/spread/pallas_call | solution.py:126
  26.5 9.7 %all-to-all-start.1 = ((bf16[32,384,256]{2,1,0:T(8,128)(2,1)}), bf16[32,384,256]{2,1,0:T(8,128)(2,1)}, u32[]{:S(2)}, u32[]{:S(2)}) async-start(bf16[32,384,256]{2,1,0:T(8,128)(2,1)} %get-tuple-element.22), calls=%async_computation.1 | async-start | bytes 12582912 | tf_op jit(solution)/shard_map/all_to_all | solution.py:420
  36.3 0.6 stack.35.dest_ref
  37.0 2.9 %copy.19.hidden_ref = bf16[1,2,8,76,1024]{4,3,2,1,0:T(8,128)(2,1)} copy(bf16[1,2,8,76,1024]{4,2,3,1,0:T(8,128)(2,1)S(1)} %copy-done.1) | data formatting | bytes 4980736 | tf_op jit(solution)/shard_map/optimization_barrier | solution.py:411
  39.8 13.0 %project.1 = (bf16[1280,256]{1,0:T(8,128)(2,1)}, bf16[1280,256]{1,0:T(8,128)(2,1)}, bf16[1280,256]{1,0:T(8,128)(2,1)}, bf16[1280,256]{1,0:T(8,128)(2,1)}, bf16[1...) custom-call(s32[8]{0:T(128)} %stack.35.dest_ref, ...), custom_call_target="tpu_custom_call" | custom-call | flops 5368709120 | bytes 11927552 | tf_op jit(solution)/shard_map/project/pallas_call | solution.py:177
  52.8 2.5 %collective-permute-start = (bf16[1280,256]{1,0:T(8,128)(2,1)}, bf16[1280,256]{1,0:T(8,128)(2,1)S(1)}, u32[]{:S(2)}, u32[]{:S(2)}) collective-permute-start(bf16[1280,256]{1,0:T(8,128)(2,1)} %get-tuple-element.25), channel_id=1, source_target_pairs={{0,1},{1,0},{2,3},{3,2},{4,5},{5,4},{6,7},{7,6},{8,9},{9,8},{10,11... | collective-permute-start | bytes 1966088 | tf_op jit(solution)/shard_map/ppermute | solution.py:422
  55.3 1.3 collective-permute-start.1
  56.6 1.5 collective-permute-start.2
  58.1 1.3 collective-permute-start.3
  59.4 3.8 %collective-permute-start.4 = (bf16[1280,256]{1,0:T(8,128)(2,1)}, bf16[1280,256]{1,0:T(8,128)(2,1)S(1)}, u32[]{:S(2)}, u32[]{:S(2)}) collective-permute-start(bf16[1280,256]{1,0:T(8,128)(2,1)} %get-tuple-element.29), channel_id=1, source_target_pairs={{0,5},{1,4},{2,7},{3,6},{4,1},{5,0},{6,3},{7,2},{8,13},{9,12},{10,... | collective-permute-start | bytes 1966088 | tf_op jit(solution)/shard_map/ppermute | solution.py:422
  63.2 19.6 %collective-permute-done.rest_1_ = bf16[1280,256]{1,0:T(8,128)(2,1)S(1)} collective-permute-done((bf16[1280,256]{1,0:T(8,128)(2,1)}, bf16[1280,256]{1,0:T(8,128)(2,1)S(1)}, u32[]{:S(2)}, u32[]{:S(2)}) %collective-permute-start) | collective-permute-done | bytes 655392 | tf_op jit(solution)/shard_map/ppermute | solution.py:422
  82.8 2.7 %collective-permute-start.5 = (bf16[1280,256]{1,0:T(8,128)(2,1)}, bf16[1280,256]{1,0:T(8,128)(2,1)S(1)}, u32[]{:S(2)}, u32[]{:S(2)}) collective-permute-start(bf16[1280,256]{1,0:T(8,128)(2,1)} %get-tuple-element.30), channel_id=1, source_target_pairs={{0,6},{1,7},{2,0},{3,1},{4,2},{5,3},{6,4},{7,5},{8,14},{9,15},{10,... | collective-permute-start | bytes 1966088 | tf_op jit(solution)/shard_map/ppermute | solution.py:422
  85.6 1.3 collective-permute-start.6
  86.9 24.6 %collective-permute-done.2.rest_3_ = bf16[1280,256]{1,0:T(8,128)(2,1)S(1)} collective-permute-done((bf16[1280,256]{1,0:T(8,128)(2,1)}, bf16[1280,256]{1,0:T(8,128)(2,1)S(1)}, u32[]{:S(2)}, u32[]{:S(2)}) %collective-permute-start.2) | collective-permute-done | bytes 655392 | tf_op jit(solution)/shard_map/ppermute | solution.py:422
  111.5 24.5 %collective-permute-done.4.rest_5_ = bf16[1280,256]{1,0:T(8,128)(2,1)S(1)} collective-permute-done((bf16[1280,256]{1,0:T(8,128)(2,1)}, bf16[1280,256]{1,0:T(8,128)(2,1)S(1)}, u32[]{:S(2)}, u32[]{:S(2)}) %collective-permute-start.4) | collective-permute-done | bytes 655392 | tf_op jit(solution)/shard_map/ppermute | solution.py:422
  135.9 27.5 %collective-permute-done.6.rest_7_ = bf16[1280,256]{1,0:T(8,128)(2,1)S(1)} collective-permute-done((bf16[1280,256]{1,0:T(8,128)(2,1)}, bf16[1280,256]{1,0:T(8,128)(2,1)S(1)}, u32[]{:S(2)}, u32[]{:S(2)}) %collective-permute-start.6) | collective-permute-done | bytes 655392 | tf_op jit(solution)/shard_map/ppermute | solution.py:422
  163.4 0.8 copy-done.8
  164.2 11.1 %attend_own.1.state_ref = f32[2,8,256,256]{3,2,1,0:T(8,128)} custom-call(bf16[1,2,256,1024]{3,2,1,0:T(8,128)(2,1)} %q_ref.5, bf16[1,2,256,128]{3,2,1,0:T(8,128)(2,1)} %nk_ref.1, bf16[1,2,256,128]{3,2,1,0:T(8,128)(2,1)} %nv_ref.1, bf16[1280,256]{1,0:T(8,128)(2,1)} %get-tuple-element.24.rest_0_, bf16[1280,256]{1,0:T(8,128)(2,1)} %copy-done.2, ...), custom_call_target="tpu_custom_call" | custom-call | flops 2818572288 | bytes 9306112 | tf_op jit(solution)/shard_map/attend_own/pallas_call | solution.py:315
  175.6 14.9 %all-to-all-start.2 = ((bf16[32,64,256]{2,1,0:T(8,128)(2,1)}), bf16[32,64,256]{2,1,0:T(8,128)(2,1)S(1)}, u32[]{:S(2)}, u32[]{:S(2)}) async-start(bf16[32,64,256]{2,1,0:T(8,128)(2,1)} %get-tuple-element.34), calls=%async_computation.2 | async-start | bytes 2097152 | tf_op jit(solution)/shard_map/all_to_all | solution.py:427
  190.5 0.6 and_select_fusion.place_ref
  191.0 21.2 %attend_main.1.state_ref = f32[2,8,256,256]{3,2,1,0:T(8,128)} custom-call(s32[16]{0:T(128)} %and_select_fusion.place_ref, bf16[1,2,256,1024]{3,2,1,0:T(8,128)(2,1)} %q_ref.5, f32[2,8,256,256]{3,2,1,0:T(8,128)} %attend_own.1.state_ref, bf16[32,384,256]{2,1,0:T(8,128)(2,1)} %all-to-all-done.1.rest_0_.rest_1_.rest_2_.rest_3_.rest_4_.rest_5_.rest_6_.rest_7_, ...), custom_call_target="tpu_custom_call" | custom-call | flops 9663676416 | bytes 11534336 | tf_op jit(solution)/shard_map/attend_main/pallas_call | solution.py:349
  212.2 4.7 %all-to-all-done.2.rest_0_.rest_1_.rest_2_.rest_3_.rest_4_.rest_5_.rest_6_.rest_7_ = bf16[32,64,256]{2,1,0:T(8,128)(2,1)S(1)} async-done(((bf16[32,64,256]{2,1,0:T(8,128)(2,1)}), bf16[32,64,256]{2,1,0:T(8,128)(2,1)S(1)}, u32[]{:S(2)}, u32[]{:S(2)}) %all-to-all-start.2) | async-done | bytes 1048608 | tf_op jit(solution)/shard_map/all_to_all | solution.py:427
  216.9 1.0 copy-done
  217.9 8.5 %attend_last.1 = bf16[1,2,256,1024]{3,2,1,0:T(8,128)(2,1)} custom-call(s32[16]{0:T(128)} %and_select_fusion.place_ref, bf16[1,2,256,1024]{3,2,1,0:T(8,128)(2,1)} %q_ref.5, f32[2,8,256,256]{3,2,1,0:T(8,128)} %attend_main.1.state_ref, bf16[32,64,256]{2,1,0:T(8,128)(2,1)} %copy-done, bf16[32,64,256]{2,1,0:T(8,128)(2,1)} %copy-done, ...), custom_call_target="tpu_custom_call" | custom-call | flops 1610612736 | bytes 8912896 | tf_op jit(solution)/shard_map/attend_last/pallas_call | solution.py:349
  (24 shorter events, 0.3 us)
Async XLA Ops:
  2.7 19.4 %all-to-all-start = ((s32[16,1,16]{2,1,0:T(1,128)}), s32[16,1,16]{2,1,0:T(1,128)S(1)}, u32[]{:S(2)}, u32[]{:S(2)}) async-start(s32[16,1,16]{2,1,0:T(1,128)} %broadcast_in_dim.26), calls=%async_computation | async-start | bytes 16384 | tf_op jit(solution)/shard_map/all_to_all | solution.py:397
  26.5 10.4 %copy-start.1 = (bf16[1,2,8,76,1024]{4,2,3,1,0:T(8,128)(2,1)S(1)}, bf16[1,2,8,76,1024]{4,2,3,1,0:T(8,128)(2,1)}, u32[]{:S(2)}) copy-start(bf16[1,2,8,76,1024]{4,2,3,1,0:T(8,128)(2,1)} %param.16) | copy-start | bytes 7471108
  26.5 149.0 %all-to-all-start.1 = ((bf16[32,384,256]{2,1,0:T(8,128)(2,1)}), bf16[32,384,256]{2,1,0:T(8,128)(2,1)}, u32[]{:S(2)}, u32[]{:S(2)}) async-start(bf16[32,384,256]{2,1,0:T(8,128)(2,1)} %get-tuple-element.22), calls=%async_computation.1 | async-start | bytes 12582912 | tf_op jit(solution)/shard_map/all_to_all | solution.py:420
  52.8 30.0 %collective-permute-start = (bf16[1280,256]{1,0:T(8,128)(2,1)}, bf16[1280,256]{1,0:T(8,128)(2,1)S(1)}, u32[]{:S(2)}, u32[]{:S(2)}) collective-permute-start(bf16[1280,256]{1,0:T(8,128)(2,1)} %get-tuple-element.25), channel_id=1, source_target_pairs={{0,1},{1,0},{2,3},{3,2},{4,5},{5,4},{6,7},{7,6},{8,9},{9,8},{10,11... | collective-permute-start | bytes 1966088 | tf_op jit(solution)/shard_map/ppermute | solution.py:422
  55.3 30.3 %collective-permute-start.1 = (bf16[1280,256]{1,0:T(8,128)(2,1)}, bf16[1280,256]{1,0:T(8,128)(2,1)S(1)}, u32[]{:S(2)}, u32[]{:S(2)}) collective-permute-start(bf16[1280,256]{1,0:T(8,128)(2,1)} %get-tuple-element.26), channel_id=1, source_target_pairs={{0,2},{1,3},{2,4},{3,5},{4,6},{5,7},{6,0},{7,1},{8,10},{9,11},{10,... | collective-permute-start | bytes 1966088 | tf_op jit(solution)/shard_map/ppermute | solution.py:422
  56.6 54.9 %collective-permute-start.2 = (bf16[1280,256]{1,0:T(8,128)(2,1)}, bf16[1280,256]{1,0:T(8,128)(2,1)S(1)}, u32[]{:S(2)}, u32[]{:S(2)}) collective-permute-start(bf16[1280,256]{1,0:T(8,128)(2,1)} %get-tuple-element.27), channel_id=1, source_target_pairs={{0,3},{1,2},{2,5},{3,4},{4,7},{5,6},{6,1},{7,0},{8,11},{9,10},{10,... | collective-permute-start | bytes 1966088 | tf_op jit(solution)/shard_map/ppermute | solution.py:422
  58.1 53.4 %collective-permute-start.3 = (bf16[1280,256]{1,0:T(8,128)(2,1)}, bf16[1280,256]{1,0:T(8,128)(2,1)S(1)}, u32[]{:S(2)}, u32[]{:S(2)}) collective-permute-start(bf16[1280,256]{1,0:T(8,128)(2,1)} %get-tuple-element.28), channel_id=1, source_target_pairs={{0,4},{1,5},{2,6},{3,7},{4,0},{5,1},{6,2},{7,3},{8,12},{9,13},{10,... | collective-permute-start | bytes 1966088 | tf_op jit(solution)/shard_map/ppermute | solution.py:422
  59.4 76.5 %collective-permute-start.4 = (bf16[1280,256]{1,0:T(8,128)(2,1)}, bf16[1280,256]{1,0:T(8,128)(2,1)S(1)}, u32[]{:S(2)}, u32[]{:S(2)}) collective-permute-start(bf16[1280,256]{1,0:T(8,128)(2,1)} %get-tuple-element.29), channel_id=1, source_target_pairs={{0,5},{1,4},{2,7},{3,6},{4,1},{5,0},{6,3},{7,2},{8,13},{9,12},{10,... | collective-permute-start | bytes 1966088 | tf_op jit(solution)/shard_map/ppermute | solution.py:422
  82.8 80.6 %copy-start.2 = (bf16[1280,256]{1,0:T(8,128)(2,1)}, bf16[1280,256]{1,0:T(8,128)(2,1)S(1)}, u32[]{:S(2)}) copy-start(bf16[1280,256]{1,0:T(8,128)(2,1)S(1)} %collective-permute-done.rest_1_) | copy-start | bytes 1966084
  82.8 53.1 %collective-permute-start.5 = (bf16[1280,256]{1,0:T(8,128)(2,1)}, bf16[1280,256]{1,0:T(8,128)(2,1)S(1)}, u32[]{:S(2)}, u32[]{:S(2)}) collective-permute-start(bf16[1280,256]{1,0:T(8,128)(2,1)} %get-tuple-element.30), channel_id=1, source_target_pairs={{0,6},{1,7},{2,0},{3,1},{4,2},{5,3},{6,4},{7,5},{8,14},{9,15},{10,... | collective-permute-start | bytes 1966088 | tf_op jit(solution)/shard_map/ppermute | solution.py:422
  85.6 77.8 %copy-start.3 = (bf16[1280,256]{1,0:T(8,128)(2,1)}, bf16[1280,256]{1,0:T(8,128)(2,1)S(1)}, u32[]{:S(2)}) copy-start(bf16[1280,256]{1,0:T(8,128)(2,1)S(1)} %collective-permute-done.1.rest_2_) | copy-start | bytes 1966084
  85.6 77.8 %collective-permute-start.6 = (bf16[1280,256]{1,0:T(8,128)(2,1)}, bf16[1280,256]{1,0:T(8,128)(2,1)S(1)}, u32[]{:S(2)}, u32[]{:S(2)}) collective-permute-start(bf16[1280,256]{1,0:T(8,128)(2,1)} %get-tuple-element.31), channel_id=1, source_target_pairs={{0,7},{1,6},{2,1},{3,0},{4,3},{5,2},{6,5},{7,4},{8,15},{9,14},{10,... | collective-permute-start | bytes 1966088 | tf_op jit(solution)/shard_map/ppermute | solution.py:422
  111.5 51.9 %copy-start.4 = (bf16[1280,256]{1,0:T(8,128)(2,1)}, bf16[1280,256]{1,0:T(8,128)(2,1)S(1)}, u32[]{:S(2)}) copy-start(bf16[1280,256]{1,0:T(8,128)(2,1)S(1)} %collective-permute-done.2.rest_3_) | copy-start | bytes 1966084
  111.5 51.9 %copy-start.5 = (bf16[1280,256]{1,0:T(8,128)(2,1)}, bf16[1280,256]{1,0:T(8,128)(2,1)S(1)}, u32[]{:S(2)}) copy-start(bf16[1280,256]{1,0:T(8,128)(2,1)S(1)} %collective-permute-done.3.rest_4_) | copy-start | bytes 1966084
  135.9 27.5 %copy-start.6 = (bf16[1280,256]{1,0:T(8,128)(2,1)}, bf16[1280,256]{1,0:T(8,128)(2,1)S(1)}, u32[]{:S(2)}) copy-start(bf16[1280,256]{1,0:T(8,128)(2,1)S(1)} %collective-permute-done.4.rest_5_) | copy-start | bytes 1966084
  135.9 27.5 %copy-start.7 = (bf16[1280,256]{1,0:T(8,128)(2,1)}, bf16[1280,256]{1,0:T(8,128)(2,1)S(1)}, u32[]{:S(2)}) copy-start(bf16[1280,256]{1,0:T(8,128)(2,1)S(1)} %collective-permute-done.5.rest_6_) | copy-start | bytes 1966084
  163.4 0.8 copy-start.8
  175.6 41.3 %all-to-all-start.2 = ((bf16[32,64,256]{2,1,0:T(8,128)(2,1)}), bf16[32,64,256]{2,1,0:T(8,128)(2,1)S(1)}, u32[]{:S(2)}, u32[]{:S(2)}) async-start(bf16[32,64,256]{2,1,0:T(8,128)(2,1)} %get-tuple-element.34), calls=%async_computation.2 | async-start | bytes 2097152 | tf_op jit(solution)/shard_map/all_to_all | solution.py:427
  216.9 1.0 copy-start

commit v4 on v3

--- a/solution.py
+++ b/solution.py
@@ -161,11 +161,13 @@
     result_ref[...] = jnp.dot(
         rows_ref[...], weight, preferred_element_type=jnp.float32
     ).astype(result_ref.dtype)
+    count = result_ref.shape[0]
     for k, out_ref in enumerate(out_refs):
-
-        @pl.when(step == k)
-        def _():
-            out_ref[...] = result_ref[...]
+        for half in range(2):
+
+            @pl.when(step == 2 * k + half)
+            def _():
+                out_ref[half * count : (half + 1) * count] = result_ref[...]
 
 
 def project(dests, hidden, w_key, w_value, slot):
@@ -174,6 +176,7 @@
     parts = dests.shape[0]
     share = w_key.shape[2] // parts
     shape = (spans * slot, 2 * share)
+    pair = (2 * spans * slot, 2 * share)
     return pl.pallas_call(
         functools.partial(project_kernel, rrows=rrows, slot=slot),
         grid_spec=pltpu.PrefetchScalarGridSpec(
@@ -184,13 +187,13 @@
                 pl.BlockSpec((1, feats, share), lambda p, to: (0, 0, to[p])),
                 pl.BlockSpec((1, feats, share), lambda p, to: (0, 0, to[p])),
             ],
-            out_specs=[pl.BlockSpec(shape, lambda p, to: (0, 0))] * parts,
+            out_specs=[pl.BlockSpec(pair, lambda p, to: (0, 0))] * (parts // 2),
             scratch_shapes=[
                 pltpu.VMEM((spans * slot, feats), jnp.bfloat16),
                 pltpu.VMEM(shape, jnp.bfloat16),
             ],
         ),
-        out_shape=[jax.ShapeDtypeStruct(shape, jnp.bfloat16)] * parts,
+        out_shape=[jax.ShapeDtypeStruct(pair, jnp.bfloat16)] * (parts // 2),
         compiler_params=pltpu.CompilerParams(vmem_limit_bytes=56 * MIB),
         cost_estimate=pl.CostEstimate(
             flops=4 * parts * spans * slot * feats * share,
@@ -310,7 +313,7 @@
     _, reqs, qlen, feats = queries.shape
     heads = feats // HD
     some = heads // 2
-    fresh_rows = pieces[0].shape[0] // reqs
+    fresh_rows = pieces[-1].shape[0] // reqs
     count = fresh_rows + qlen
     return pl.pallas_call(
         functools.partial(own_kernel, rrows=rrows, slot=slot),
@@ -419,9 +422,14 @@
     partial = project(dests, hidden, w_key, w_value, slot)
     arrived = lax.all_to_all(main, ("section", "dp"), 0, 0, tiled=True)
     pieces = [partial[0]] + [
-        lax.ppermute(piece, "tensor", [(i, moved(i, move)) for i in range(parts)])
-        for piece, move in zip(partial[1:], moves[1:])
+        lax.ppermute(piece, "tensor", [(i, moved(i, (shift, 0))) for i in range(parts)])
+        for shift, piece in enumerate(partial[1:], 1)
     ]
+    count = req_dev * topk * slot
+    across = sum(piece[count:].astype(jnp.float32) for piece in pieces).astype(jnp.bfloat16)
+    pieces.append(
+        lax.ppermute(across, "tensor", [(i, moved(i, (0, 1))) for i in range(parts)])
+    )
     state = attend_own(queries, pieces, query_keys, query_values, rrows, slot)
     rest, arrived, state = lax.optimization_barrier((rest, arrived, state))
     arrived_rest = lax.all_to_all(rest, ("section", "dp"), 0, 0, tiled=True)

time: 228 us -> 222 us (0.974)
  starting transfers between devices: 49 us -> 33.7 us
  waiting for transfers between devices: 101 us -> 107 us
    all_to_all x1, waiting for transfers between devices: 0.2 us -> 21.7 us  [on_device(): arrived = lax.all_to_all(main, ('section', 'dp'), 0, 0, tiled=True)]
    ppermute x7 -> x4, waiting for transfers between devices: 96.1 us -> 80.4 us  [the longest x3 55.9 us: on_device(): lax.ppermute(piece, 'tensor', [(i, moved(i, (shift, 0))) for i in range(p...]
    ppermute x7 -> x4, starting transfers between devices: 14.5 us -> 7.51 us  [the longest x3 4.98 us: on_device(): lax.ppermute(piece, 'tensor', [(i, moved(i, (shift, 0))) for i in range(p...]
    all_to_all x1, starting transfers between devices: 14.9 us -> 8.95 us  [on_device(): arrived_rest = lax.all_to_all(rest, ('section', 'dp'), 0, 0, tiled=True)]
    all_to_all x1, starting transfers between devices: 9.67 us -> 7.23 us  [on_device(): arrived = lax.all_to_all(main, ('section', 'dp'), 0, 0, tiled=True)]
  transfers between devices with their start and end apart: 10 -> 7, of which waited for: 6 -> 5; matrix products, arithmetic and copies ran while one was open for 3% -> 4% of each run, Pallas kernels for 23% -> 23%
where the time goes in v4:
time: 222 us; the launch traced here: 220 us
  waiting for transfers between devices  107 us (48%)
  Pallas kernels  64.9 us (29%)
  starting transfers between devices  33.7 us (15%)
  local copies, waits for them, and re-layouts  9.07 us (4%)
  other arithmetic  5.16 us (2%)
    ppermute x3, waiting for transfers between devices, on_device(): lax.ppermute(piece, 'tensor', [(i, moved(i, (shift, 0))) for i in range(p...  55.9 us
    pallas_call x2, Pallas kernels, attend_spans(): pl.pallas_call(functools.partial(last_kernel, kept=kept) if last else mai...  29.7 us
    ppermute x1, waiting for transfers between devices, on_device(): lax.ppermute(across, 'tensor', [(i, moved(i, (0, 1))) for i in range(part...  24.5 us
    all_to_all x1, waiting for transfers between devices, on_device(): arrived = lax.all_to_all(main, ('section', 'dp'), 0, 0, tiled=True)  21.7 us
    pallas_call x1, Pallas kernels, project(): pl.pallas_call(functools.partial(project_kernel, rrows=rrows, slot=slot),...  13 us
    pallas_call x1, Pallas kernels, attend_own(): pl.pallas_call(functools.partial(own_kernel, rrows=rrows, slot=slot), gri...  10.3 us
    all_to_all x1, starting transfers between devices, on_device(): lax.all_to_all(jnp.broadcast_to(own_slot[None], (groups, req_dev * topk))...  9.98 us
    all_to_all x1, starting transfers between devices, on_device(): arrived_rest = lax.all_to_all(rest, ('section', 'dp'), 0, 0, tiled=True)  8.95 us
  transfers between devices with their start and end apart: 7, of which 5 were waited for; matrix products, arithmetic and copies ran while one was open for 4% of the time, Pallas kernels for 23%

profile of v4, /device:TPU:1, one launch (start us, length us, event | category | flops | bytes accessed | tf_op | source)
XLA Modules:
  0.0 219.9 jit_solution(1047409501935415191)
XLA Ops:
  0.0 0.7 compare_select_fusion
  0.7 0.1 reshape.19
  0.8 1.3 gather_fusion
  2.1 0.6 broadcast_in_dim.26
  2.7 10.0 %all-to-all-start = ((s32[16,1,16]{2,1,0:T(1,128)}), s32[16,1,16]{2,1,0:T(1,128)S(1)}, u32[]{:S(2)}, u32[]{:S(2)}) async-start(s32[16,1,16]{2,1,0:T(1,128)} %broadcast_in_dim.26), calls=%async_computation | async-start | bytes 16384 | tf_op jit(solution)/shard_map/all_to_all | solution.py:400
  12.7 1.4 select_reduce_fusion.ids_ref
  14.1 1.6 copy.18.rows_ref
  15.8 6.4 %compact.1.packed_ref = bf16[2,8,448,256]{3,2,1,0:T(8,128)(2,1)} custom-call(s32[8]{0:T(128)} %select_reduce_fusion.ids_ref, s32[256,76]{1,0:T(8,128)} %copy.18.rows_ref, bf16[2,8,512,128]{3,2,1,0:T(8,128)(2,1)} %ck_ref.1, bf16[2,8,512,128]{3,2,1,0:T(8,128)(2,1)} %cv_ref.1), custom_call_target="tpu_custom_call" | custom-call | flops 1879048192 | bytes 8388608 | tf_op jit(solution)/shard_map/compact/pallas_call | solution.py:59
  22.2 0.6 fusion.2.local_ref
  22.8 5.5 %spread.1 = (bf16[32,384,256]{2,1,0:T(8,128)(2,1)}, bf16[32,64,256]{2,1,0:T(8,128)(2,1)}) custom-call(s32[16]{0:T(128)} %fusion.2.local_ref, bf16[2,8,448,256]{3,2,1,0:T(8,128)(2,1)} %compact.1.packed_ref), custom_call_target="tpu_custom_call" | custom-call | bytes 11010048 | tf_op jit(solution)/shard_map/spread/pallas_call | solution.py:126
  28.4 0.0 copy-start.4
  28.4 7.2 %all-to-all-start.1 = ((bf16[32,384,256]{2,1,0:T(8,128)(2,1)}), bf16[32,384,256]{2,1,0:T(8,128)(2,1)}, u32[]{:S(2)}, u32[]{:S(2)}) async-start(bf16[32,384,256]{2,1,0:T(8,128)(2,1)} %get-tuple-element.18), calls=%async_computation.1 | async-start | bytes 12582912 | tf_op jit(solution)/shard_map/all_to_all | solution.py:423
  35.7 0.7 stack.35.dest_ref
  36.4 2.9 %copy.19.hidden_ref = bf16[1,2,8,76,1024]{4,3,2,1,0:T(8,128)(2,1)} copy(bf16[1,2,8,76,1024]{4,2,3,1,0:T(8,128)(2,1)S(1)} %copy-done.4) | data formatting | bytes 4980736 | tf_op jit(solution)/shard_map/optimization_barrier | solution.py:414
  39.3 13.0 %project.1 = (bf16[2560,256]{1,0:T(8,128)(2,1)}, bf16[2560,256]{1,0:T(8,128)(2,1)}, bf16[2560,256]{1,0:T(8,128)(2,1)}, bf16[2560,256]{1,0:T(8,128)(2,1)}) custom-call(s32[8]{0:T(128)} %stack.35.dest_ref, bf16[1,2,8,76,1024]{4,3,2,1,0:T(8,128)(2,1)} %copy.19.hidden_ref, bf16[1,1024,1024]{2,1,0:T(8,128)(2,1)} %wk_ref.1, bf16[1,1024,1024]{2,1,0:T(8,128)(2,1)} %wv_ref.1), custom_call_target="tpu_custom_call" | custom-call | flops 5368709120 | bytes 11927552 | tf_op jit(solution)/shard_map/project/pallas_call | solution.py:180
  52.3 1.3 collective-permute-start
  53.6 2.6 %collective-permute-start.1 = (bf16[2560,256]{1,0:T(8,128)(2,1)}, bf16[2560,256]{1,0:T(8,128)(2,1)S(1)}, u32[]{:S(2)}, u32[]{:S(2)}) collective-permute-start(bf16[2560,256]{1,0:T(8,128)(2,1)} %get-tuple-element.22), channel_id=1, source_target_pairs={{0,4},{1,5},{2,6},{3,7},{4,0},{5,1},{6,2},{7,3},{8,12},{9,13},{10,... | collective-permute-start | bytes 3932168 | tf_op jit(solution)/shard_map/ppermute | solution.py:425
  56.2 1.1 collective-permute-start.2
  57.2 26.7 %collective-permute-done.rest_1_ = bf16[2560,256]{1,0:T(8,128)(2,1)S(1)} collective-permute-done((bf16[2560,256]{1,0:T(8,128)(2,1)}, bf16[2560,256]{1,0:T(8,128)(2,1)S(1)}, u32[]{:S(2)}, u32[]{:S(2)}) %collective-permute-start) | collective-permute-done | bytes 1310752 | tf_op jit(solution)/shard_map/ppermute | solution.py:425
  84.0 29.2 %collective-permute-done.1.rest_2_ = bf16[2560,256]{1,0:T(8,128)(2,1)S(1)} collective-permute-done((bf16[2560,256]{1,0:T(8,128)(2,1)}, bf16[2560,256]{1,0:T(8,128)(2,1)S(1)}, u32[]{:S(2)}, u32[]{:S(2)}) %collective-permute-start.1) | collective-permute-done | bytes 1310752 | tf_op jit(solution)/shard_map/ppermute | solution.py:425
  113.2 1.9 add_convert_fusion
  115.1 2.5 %collective-permute-start.3 = (bf16[1280,256]{1,0:T(8,128)(2,1)S(1)}, bf16[1280,256]{1,0:T(8,128)(2,1)S(1)}, u32[]{:S(2)}, u32[]{:S(2)}) collective-permute-start(bf16[1280,256]{1,0:T(8,128)(2,1)S(1)} %add_convert_fusion), channel_id=1, source_target_pairs={{0,1},{1,0},{2,3},{3,2},{4,5},{5,4},{6,7},{7,6},{8,9},{9,8},{10,11... | collective-permute-start | bytes 1966088 | tf_op jit(solution)/shard_map/ppermute | solution.py:431
  117.6 24.5 %collective-permute-done.3.rest_4_ = bf16[1280,256]{1,0:T(8,128)(2,1)S(1)} collective-permute-done((bf16[1280,256]{1,0:T(8,128)(2,1)S(1)}, bf16[1280,256]{1,0:T(8,128)(2,1)S(1)}, u32[]{:S(2)}, u32[]{:S(2)}) %collective-permute-start.3) | collective-permute-done | bytes 655392 | tf_op jit(solution)/shard_map/ppermute | solution.py:431
  142.1 0.9 copy-done.5
  143.0 10.3 %attend_own.1.state_ref = f32[2,8,256,256]{3,2,1,0:T(8,128)} custom-call(bf16[1,2,256,1024]{3,2,1,0:T(8,128)(2,1)} %q_ref.5, bf16[1,2,256,128]{3,2,1,0:T(8,128)(2,1)} %nk_ref.1, bf16[1,2,256,128]{3,2,1,0:T(8,128)(2,1)} %nv_ref.1, bf16[2560,256]{1,0:T(8,128)(2,1)} %get-tuple-element.20.rest_0_, bf16[2560,256]{1,0:T(8,128)(2,1)} %copy-done.1, ...), custom_call_target="tpu_custom_call" | custom-call | flops 2818572288 | bytes 9306112 | tf_op jit(solution)/shard_map/attend_own/pallas_call | solution.py:318
  153.3 21.7 %all-to-all-done.1.rest_0_.rest_1_.rest_2_.rest_3_.rest_4_.rest_5_.rest_6_.rest_7_ = bf16[32,384,256]{2,1,0:T(8,128)(2,1)} async-done(((bf16[32,384,256]{2,1,0:T(8,128)(2,1)}), bf16[32,384,256]{2,1,0:T(8,128)(2,1)}, u32[]{:S(2)}, u32[]{:S(2)}) %all-to-all-start.1) | async-done | bytes 6291488 | tf_op jit(solution)/shard_map/all_to_all | solution.py:423
  175.0 9.0 %all-to-all-start.2 = ((bf16[32,64,256]{2,1,0:T(8,128)(2,1)}), bf16[32,64,256]{2,1,0:T(8,128)(2,1)S(1)}, u32[]{:S(2)}, u32[]{:S(2)}) async-start(bf16[32,64,256]{2,1,0:T(8,128)(2,1)} %get-tuple-element.26), calls=%async_computation.2 | async-start | bytes 2097152 | tf_op jit(solution)/shard_map/all_to_all | solution.py:435
  183.9 0.5 and_select_fusion.place_ref
  184.5 21.2 %attend_main.1.state_ref = f32[2,8,256,256]{3,2,1,0:T(8,128)} custom-call(s32[16]{0:T(128)} %and_select_fusion.place_ref, bf16[1,2,256,1024]{3,2,1,0:T(8,128)(2,1)} %q_ref.5, f32[2,8,256,256]{3,2,1,0:T(8,128)} %attend_own.1.state_ref, bf16[32,384,256]{2,1,0:T(8,128)(2,1)} %all-to-all-done.1.rest_0_.rest_1_.rest_2_.rest_3_.rest_4_.rest_5_.rest_6_.rest_7_, ...), custom_call_target="tpu_custom_call" | custom-call | flops 9663676416 | bytes 11534336 | tf_op jit(solution)/shard_map/attend_main/pallas_call | solution.py:352
  205.6 4.7 %all-to-all-done.2.rest_0_.rest_1_.rest_2_.rest_3_.rest_4_.rest_5_.rest_6_.rest_7_ = bf16[32,64,256]{2,1,0:T(8,128)(2,1)S(1)} async-done(((bf16[32,64,256]{2,1,0:T(8,128)(2,1)}), bf16[32,64,256]{2,1,0:T(8,128)(2,1)S(1)}, u32[]{:S(2)}, u32[]{:S(2)}) %all-to-all-start.2) | async-done | bytes 1048608 | tf_op jit(solution)/shard_map/all_to_all | solution.py:435
  210.4 1.0 copy-done
  211.3 8.5 %attend_last.1 = bf16[1,2,256,1024]{3,2,1,0:T(8,128)(2,1)} custom-call(s32[16]{0:T(128)} %and_select_fusion.place_ref, bf16[1,2,256,1024]{3,2,1,0:T(8,128)(2,1)} %q_ref.5, f32[2,8,256,256]{3,2,1,0:T(8,128)} %attend_main.1.state_ref, bf16[32,64,256]{2,1,0:T(8,128)(2,1)} %copy-done, bf16[32,64,256]{2,1,0:T(8,128)(2,1)} %copy-done, ...), custom_call_target="tpu_custom_call" | custom-call | flops 1610612736 | bytes 8912896 | tf_op jit(solution)/shard_map/attend_last/pallas_call | solution.py:352
  (13 shorter events, 0.0 us)
Async XLA Ops:
  2.7 19.5 %all-to-all-start = ((s32[16,1,16]{2,1,0:T(1,128)}), s32[16,1,16]{2,1,0:T(1,128)S(1)}, u32[]{:S(2)}, u32[]{:S(2)}) async-start(s32[16,1,16]{2,1,0:T(1,128)} %broadcast_in_dim.26), calls=%async_computation | async-start | bytes 16384 | tf_op jit(solution)/shard_map/all_to_all | solution.py:400
  28.4 8.0 %copy-start.4 = (bf16[1,2,8,76,1024]{4,2,3,1,0:T(8,128)(2,1)S(1)}, bf16[1,2,8,76,1024]{4,2,3,1,0:T(8,128)(2,1)}, u32[]{:S(2)}) copy-start(bf16[1,2,8,76,1024]{4,2,3,1,0:T(8,128)(2,1)} %param.16) | copy-start | bytes 7471108
  28.4 146.6 %all-to-all-start.1 = ((bf16[32,384,256]{2,1,0:T(8,128)(2,1)}), bf16[32,384,256]{2,1,0:T(8,128)(2,1)}, u32[]{:S(2)}, u32[]{:S(2)}) async-start(bf16[32,384,256]{2,1,0:T(8,128)(2,1)} %get-tuple-element.18), calls=%async_computation.1 | async-start | bytes 12582912 | tf_op jit(solution)/shard_map/all_to_all | solution.py:423
  52.3 31.7 %collective-permute-start = (bf16[2560,256]{1,0:T(8,128)(2,1)}, bf16[2560,256]{1,0:T(8,128)(2,1)S(1)}, u32[]{:S(2)}, u32[]{:S(2)}) collective-permute-start(bf16[2560,256]{1,0:T(8,128)(2,1)} %get-tuple-element.21), channel_id=1, source_target_pairs={{0,2},{1,3},{2,4},{3,5},{4,6},{5,7},{6,0},{7,1},{8,10},{9,11},{10,... | collective-permute-start | bytes 3932168 | tf_op jit(solution)/shard_map/ppermute | solution.py:425
  53.6 59.6 %collective-permute-start.1 = (bf16[2560,256]{1,0:T(8,128)(2,1)}, bf16[2560,256]{1,0:T(8,128)(2,1)S(1)}, u32[]{:S(2)}, u32[]{:S(2)}) collective-permute-start(bf16[2560,256]{1,0:T(8,128)(2,1)} %get-tuple-element.22), channel_id=1, source_target_pairs={{0,4},{1,5},{2,6},{3,7},{4,0},{5,1},{6,2},{7,3},{8,12},{9,13},{10,... | collective-permute-start | bytes 3932168 | tf_op jit(solution)/shard_map/ppermute | solution.py:425
  56.2 57.0 %collective-permute-start.2 = (bf16[2560,256]{1,0:T(8,128)(2,1)}, bf16[2560,256]{1,0:T(8,128)(2,1)S(1)}, u32[]{:S(2)}, u32[]{:S(2)}) collective-permute-start(bf16[2560,256]{1,0:T(8,128)(2,1)} %get-tuple-element.23), channel_id=1, source_target_pairs={{0,6},{1,7},{2,0},{3,1},{4,2},{5,3},{6,4},{7,5},{8,14},{9,15},{10,... | collective-permute-start | bytes 3932168 | tf_op jit(solution)/shard_map/ppermute | solution.py:425
  84.0 31.1 %copy-start.1 = (bf16[2560,256]{1,0:T(8,128)(2,1)}, bf16[2560,256]{1,0:T(8,128)(2,1)S(1)}, u32[]{:S(2)}) copy-start(bf16[2560,256]{1,0:T(8,128)(2,1)S(1)} %collective-permute-done.rest_1_) | copy-start | bytes 3932164
  113.2 1.9 copy-start.2
  113.2 28.9 %copy-start.3 = (bf16[2560,256]{1,0:T(8,128)(2,1)}, bf16[2560,256]{1,0:T(8,128)(2,1)S(1)}, u32[]{:S(2)}) copy-start(bf16[2560,256]{1,0:T(8,128)(2,1)S(1)} %collective-permute-done.2.rest_3_) | copy-start | bytes 3932164
  115.1 27.0 %collective-permute-start.3 = (bf16[1280,256]{1,0:T(8,128)(2,1)S(1)}, bf16[1280,256]{1,0:T(8,128)(2,1)S(1)}, u32[]{:S(2)}, u32[]{:S(2)}) collective-permute-start(bf16[1280,256]{1,0:T(8,128)(2,1)S(1)} %add_convert_fusion), channel_id=1, source_target_pairs={{0,1},{1,0},{2,3},{3,2},{4,5},{5,4},{6,7},{7,6},{8,9},{9,8},{10,11... | collective-permute-start | bytes 1966088 | tf_op jit(solution)/shard_map/ppermute | solution.py:431
  142.1 0.9 copy-start.5
  175.0 35.4 %all-to-all-start.2 = ((bf16[32,64,256]{2,1,0:T(8,128)(2,1)}), bf16[32,64,256]{2,1,0:T(8,128)(2,1)S(1)}, u32[]{:S(2)}, u32[]{:S(2)}) async-start(bf16[32,64,256]{2,1,0:T(8,128)(2,1)} %get-tuple-element.26), calls=%async_computation.2 | async-start | bytes 2097152 | tf_op jit(solution)/shard_map/all_to_all | solution.py:435
  210.4 1.0 copy-start

commit v5 on v4

--- a/solution.py
+++ b/solution.py
@@ -20,7 +20,7 @@
 def compact_kernel(ids_ref, rows_ref, ck_ref, cv_ref, out_ref, *, kept):
     layers, some, clen, width = ck_ref.shape
     padded = out_ref.shape[2]
-    rr = rows_ref.shape[1]
+    rr, all_spans = rows_ref.shape
     earlier = (
         lax.broadcasted_iota(jnp.int32, (clen, clen), 0)
         < lax.broadcasted_iota(jnp.int32, (clen, clen), 1)
@@ -30,11 +30,11 @@
     target = jnp.where(target < kept, target, 0)
     keeps = []
     for i in range(some):
-        rows = rows_ref[pl.ds(ids_ref[pl.program_id(0) * some + i], 1), :]
-        hit = (lax.broadcasted_iota(jnp.int32, (clen, rr), 0) == rows).astype(jnp.bfloat16)
-        gone = lax.dot_general(
-            ones, hit, (((1,), (1,)), ((), ())), preferred_element_type=jnp.float32
-        )
+        span = ids_ref[pl.program_id(0) * some + i]
+        this = lax.broadcasted_iota(jnp.int32, (rr, all_spans), 1) == span
+        rows = jnp.sum(jnp.where(this, rows_ref[...], 0), axis=1, keepdims=True)
+        hit = (lax.broadcasted_iota(jnp.int32, (rr, clen), 1) == rows).astype(jnp.bfloat16)
+        gone = jnp.dot(ones, hit, preferred_element_type=jnp.float32)
         keeps.append(1.0 - gone)
     ranks = jnp.dot(
         jnp.concatenate(keeps, axis=0).astype(jnp.bfloat16),
@@ -285,20 +285,35 @@
         out_ref[0, h] = pack_state(*attend_head(q, key_ref, wide_ref, state_ref[0, h], None))
 
 
-def last_kernel(place_ref, q_ref, state_ref, *rest, kept):
-    out_ref, key_ref, wide_ref = rest[-3:]
-    blocks = rest[:-3]
-
-    @pl.when(pl.program_id(1) == 0)
-    def _():
-        gather_keys(blocks, key_ref, wide_ref, kept)
-
-    for h in range(state_ref.shape[1]):
-        lanes = slice(h * HD, (h + 1) * HD)
-        total, _ = attend_head(
-            q_ref[0, 0, :, lanes], key_ref, wide_ref, state_ref[0, h], None
-        )
-        out_ref[0, 0, :, lanes] = (total[:, :HD] / total[:, HD : HD + 1]).astype(out_ref.dtype)
+def last_kernel(
+    place_ref, q_ref, state_ref, arrived_ref, out_ref, key_ref, wide_ref, done_ref, sem, *, kept
+):
+    _, reqs, _, feats = q_ref.shape
+    topk = place_ref.shape[0] // reqs
+    rows = arrived_ref.shape[1]
+    real = lax.broadcasted_iota(jnp.int32, (rows, HD), 0) < kept
+    copies = []
+    for r in range(reqs):
+        for j in range(topk):
+            span = slice(j * rows, (j + 1) * rows)
+            block = arrived_ref[place_ref[r * topk + j]]
+            key_ref[r, span] = block[:, :HD]
+            wide_ref[r, span, :HD] = jnp.where(real, block[:, HD:], 0).astype(jnp.bfloat16)
+            wide_ref[r, span, HD:] = real.astype(jnp.bfloat16)
+    for r in range(reqs):
+        for h in range(feats // HD):
+            lanes = slice(h * HD, (h + 1) * HD)
+            total, _ = attend_head(
+                q_ref[0, r, :, lanes], key_ref.at[r], wide_ref.at[r], state_ref[r, h], None
+            )
+            done_ref[r, :, lanes] = (total[:, :HD] / total[:, HD : HD + 1]).astype(
+                done_ref.dtype
+            )
+        copy = pltpu.make_async_copy(done_ref.at[r], out_ref.at[0, r], sem.at[r])
+        copy.start()
+        copies.append(copy)
+    for copy in copies:
+        copy.wait()
 
 
 def attend_cost(reqs, heads, qlen, count):
@@ -336,38 +351,60 @@
     )(queries, query_keys, query_values, *pieces)
 
 
-def attend_spans(place, queries, state, arrived, kept, last):
+def attend_main(place, queries, state, arrived):
     _, reqs, qlen, feats = queries.shape
     heads = feats // HD
-    some = heads
     rows = arrived.shape[1]
     topk = place.shape[0] // reqs
     count = topk * rows
-    q_spec = pl.BlockSpec((1, 1, qlen, some * HD), lambda r, h, at: (0, r, 0, h))
-    state_spec = pl.BlockSpec((1, some, qlen, 2 * HD), lambda r, h, at: (r, h, 0, 0))
+    state_spec = pl.BlockSpec((1, heads, qlen, 2 * HD), lambda r, h, at: (r, h, 0, 0))
     blocks = [
         pl.BlockSpec((1, rows, 2 * HD), lambda r, h, at, j=j: (at[r * topk + j], 0, 0))
         for j in range(topk)
     ]
     return pl.pallas_call(
-        functools.partial(last_kernel, kept=kept) if last else main_kernel,
+        main_kernel,
         grid_spec=pltpu.PrefetchScalarGridSpec(
             num_scalar_prefetch=1,
-            grid=(reqs, heads // some),
-            in_specs=[q_spec, state_spec] + blocks,
-            out_specs=q_spec if last else state_spec,
+            grid=(reqs, 1),
+            in_specs=[
+                pl.BlockSpec((1, 1, qlen, feats), lambda r, h, at: (0, r, 0, h)),
+                state_spec,
+            ]
+            + blocks,
+            out_specs=state_spec,
             scratch_shapes=[
                 pltpu.VMEM((count, HD), jnp.bfloat16),
                 pltpu.VMEM((count, 2 * HD), jnp.bfloat16),
             ],
         ),
-        out_shape=jax.ShapeDtypeStruct(queries.shape, jnp.bfloat16)
-        if last
-        else jax.ShapeDtypeStruct(state.shape, state.dtype),
+        out_shape=jax.ShapeDtypeStruct(state.shape, state.dtype),
         compiler_params=pltpu.CompilerParams(vmem_limit_bytes=56 * MIB),
         cost_estimate=attend_cost(reqs, heads, qlen, count),
-        name="attend_last" if last else "attend_main",
+        name="attend_main",
     )(place, queries, state, *([arrived] * topk))
+
+
+def attend_last(place, queries, state, arrived, kept):
+    _, reqs, qlen, feats = queries.shape
+    heads = feats // HD
+    count = place.shape[0] // reqs * arrived.shape[1]
+    whole = pl.BlockSpec(memory_space=pltpu.VMEM)
+    return pl.pallas_call(
+        functools.partial(last_kernel, kept=kept),
+        in_specs=[pl.BlockSpec(memory_space=pltpu.SMEM), whole, whole, whole],
+        out_specs=pl.BlockSpec(memory_space=pl.ANY),
+        out_shape=jax.ShapeDtypeStruct(queries.shape, jnp.bfloat16),
+        scratch_shapes=[
+            pltpu.VMEM((reqs, count, HD), jnp.bfloat16),
+            pltpu.VMEM((reqs, count, 2 * HD), jnp.bfloat16),
+            pltpu.VMEM((reqs, qlen, feats), jnp.bfloat16),
+            pltpu.SemaphoreType.DMA((reqs,)),
+        ],
+        compiler_params=pltpu.CompilerParams(vmem_limit_bytes=32 * MIB),
+        cost_estimate=attend_cost(reqs, heads, qlen, count),
+        name="attend_last",
+    )(place, queries, state, arrived)
 
 
 def on_device(
@@ -391,8 +428,8 @@
     req_dev, topk = span_ids.shape
     rrows = hidden.shape[3]
     kept = clen - rrows
-    cut = kept // HD * HD
-    padded = ceil_to(kept, 64)
+    padded = ceil_to(kept, TILE)
+    cut = padded - 3 * TILE
     slot = ceil_to(rrows, TILE)
     myself = lax.axis_index("section") * groups + lax.axis_index("dp")
 
@@ -406,7 +443,7 @@
     ids = jnp.sum(
         jnp.where(held, jnp.arange(owner_slot.shape[0], dtype=jnp.int32)[None], 0), axis=1
     )
-    packed = compact(ids, recompute_rows, cache_keys, cache_values, kept, padded)
+    packed = compact(ids, recompute_rows.T, cache_keys, cache_values, kept, padded)
 
     mine = every_slot // per_owner == myself
     local = jnp.max(jnp.where(mine, every_slot % per_owner, -1), axis=1)
@@ -435,8 +472,8 @@
     arrived_rest = lax.all_to_all(rest, ("section", "dp"), 0, 0, tiled=True)
 
     place = own_slot // per_owner
-    state = attend_spans(place, queries, state, arrived, cut, False)
-    return attend_spans(place, queries, state, arrived_rest, kept - cut, True)
+    state = attend_main(place, queries, state, arrived)
+    return attend_last(place, queries, state, arrived_rest, kept - cut)
 
 
 def solution(mesh):

time: 222 us -> 221 us (level)
  Pallas kernels: 64.9 us -> 62.5 us
    all_to_all x1, waiting for transfers between devices: 21.7 us -> 27.3 us  [on_device(): arrived = lax.all_to_all(main, ('section', 'dp'), 0, 0, tiled=True)]
    all_to_all x1, waiting for transfers between devices: 4.73 us -> 0.01 us  [on_device(): arrived_rest = lax.all_to_all(rest, ('section', 'dp'), 0, 0, tiled=True)]
  transfers between devices with their start and end apart: 7 -> 7, of which waited for: 5 -> 4; matrix products, arithmetic and copies ran while one was open for 4% -> 3% of each run, Pallas kernels for 23% -> 24%
where the time goes in v5:
time: 221 us; the launch traced here: 220 us
  waiting for transfers between devices  108 us (49%)
  Pallas kernels  62.5 us (28%)
  starting transfers between devices  35.4 us (16%)
  local copies, waits for them, and re-layouts  8.55 us (4%)
  other arithmetic  5.24 us (2%)
    ppermute x3, waiting for transfers between devices, on_device(): lax.ppermute(piece, 'tensor', [(i, moved(i, (shift, 0))) for i in range(p...  55.9 us
    all_to_all x1, waiting for transfers between devices, on_device(): arrived = lax.all_to_all(main, ('section', 'dp'), 0, 0, tiled=True)  27.3 us
    ppermute x1, waiting for transfers between devices, on_device(): lax.ppermute(across, 'tensor', [(i, moved(i, (0, 1))) for i in range(part...  24.5 us
    pallas_call x1, Pallas kernels, attend_main(): pl.pallas_call(main_kernel, grid_spec=pltpu.PrefetchScalarGridSpec(num_sc...  21.9 us
    pallas_call x1, Pallas kernels, project(): pl.pallas_call(functools.partial(project_kernel, rrows=rrows, slot=slot),...  13 us
    pallas_call x1, Pallas kernels, attend_own(): pl.pallas_call(functools.partial(own_kernel, rrows=rrows, slot=slot), gri...  10.3 us
    all_to_all x1, starting transfers between devices, on_device(): lax.all_to_all(jnp.broadcast_to(own_slot[None], (groups, req_dev * topk))...  9.98 us
    all_to_all x1, starting transfers between devices, on_device(): arrived_rest = lax.all_to_all(rest, ('section', 'dp'), 0, 0, tiled=True)  9.12 us
  transfers between devices with their start and end apart: 7, of which 4 were waited for; matrix products, arithmetic and copies ran while one was open for 3% of the time, Pallas kernels for 24%

profile of v5, /device:TPU:1, one launch (start us, length us, event | category | flops | bytes accessed | tf_op | source)
XLA Modules:
  0.0 219.9 jit_solution(6593487244029064985)
XLA Ops:
  0.0 0.7 compare_select_fusion
  0.7 0.1 reshape.19
  0.8 1.3 gather_fusion
  2.1 0.6 broadcast_in_dim.26
  2.7 10.0 %all-to-all-start = ((s32[16,1,16]{2,1,0:T(1,128)}), s32[16,1,16]{2,1,0:T(1,128)S(1)}, u32[]{:S(2)}, u32[]{:S(2)}) async-start(s32[16,1,16]{2,1,0:T(1,128)} %broadcast_in_dim.26), calls=%async_computation | async-start | bytes 16384 | tf_op jit(solution)/shard_map/all_to_all | solution.py:437
  12.7 1.4 select_reduce_fusion.ids_ref
  14.2 6.5 %compact.1.packed_ref = bf16[2,8,448,256]{3,2,1,0:T(8,128)(2,1)} custom-call(s32[8]{0:T(128)} %select_reduce_fusion.ids_ref, s32[76,256]{1,0:T(8,128)} %bitcast.10, bf16[2,8,512,128]{3,2,1,0:T(8,128)(2,1)} %ck_ref.1, bf16[2,8,512,128]{3,2,1,0:T(8,128)(2,1)} %cv_ref.1), custom_call_target="tpu_custom_call" | custom-call | flops 1879048192 | bytes 8388608 | tf_op jit(solution)/shard_map/compact/pallas_call | solution.py:59
  20.6 0.0 all-to-all-done
  20.7 0.7 fusion.2.local_ref
  21.4 4.9 %spread.1 = (bf16[32,400,256]{2,1,0:T(8,128)(2,1)}, bf16[32,48,256]{2,1,0:T(8,128)(2,1)}) custom-call(s32[16]{0:T(128)} %fusion.2.local_ref, bf16[2,8,448,256]{3,2,1,0:T(8,128)(2,1)} %compact.1.packed_ref), custom_call_target="tpu_custom_call" | custom-call | bytes 11010048 | tf_op jit(solution)/shard_map/spread/pallas_call | solution.py:126
  26.3 0.0 copy-start.6
  26.3 8.8 %all-to-all-start.1 = ((bf16[32,400,256]{2,1,0:T(8,128)(2,1)}), bf16[32,400,256]{2,1,0:T(8,128)(2,1)}, u32[]{:S(2)}, u32[]{:S(2)}) async-start(bf16[32,400,256]{2,1,0:T(8,128)(2,1)} %get-tuple-element.18), calls=%async_computation.1 | async-start | bytes 13107200 | tf_op jit(solution)/shard_map/all_to_all | solution.py:460
  35.1 0.6 stack.35.dest_ref
  35.8 2.8 %copy.15.hidden_ref = bf16[1,2,8,76,1024]{4,3,2,1,0:T(8,128)(2,1)} copy(bf16[1,2,8,76,1024]{4,2,3,1,0:T(8,128)(2,1)S(1)} %copy-done.6) | data formatting | bytes 4980736 | tf_op jit(solution)/shard_map/optimization_barrier | solution.py:451
  38.6 13.0 %project.1 = (bf16[2560,256]{1,0:T(8,128)(2,1)}, bf16[2560,256]{1,0:T(8,128)(2,1)}, bf16[2560,256]{1,0:T(8,128)(2,1)}, bf16[2560,256]{1,0:T(8,128)(2,1)}) custom-call(s32[8]{0:T(128)} %stack.35.dest_ref, bf16[1,2,8,76,1024]{4,3,2,1,0:T(8,128)(2,1)} %copy.15.hidden_ref, bf16[1,1024,1024]{2,1,0:T(8,128)(2,1)} %wk_ref.1, bf16[1,1024,1024]{2,1,0:T(8,128)(2,1)} %wv_ref.1), custom_call_target="tpu_custom_call" | custom-call | flops 5368709120 | bytes 11927552 | tf_op jit(solution)/shard_map/project/pallas_call | solution.py:180
  51.6 1.3 collective-permute-start
  52.9 2.6 %collective-permute-start.1 = (bf16[2560,256]{1,0:T(8,128)(2,1)}, bf16[2560,256]{1,0:T(8,128)(2,1)S(1)}, u32[]{:S(2)}, u32[]{:S(2)}) collective-permute-start(bf16[2560,256]{1,0:T(8,128)(2,1)} %get-tuple-element.22), channel_id=1, source_target_pairs={{0,4},{1,5},{2,6},{3,7},{4,0},{5,1},{6,2},{7,3},{8,12},{9,13},{10,... | collective-permute-start | bytes 3932168 | tf_op jit(solution)/shard_map/ppermute | solution.py:462
  55.5 1.1 collective-permute-start.2
  56.6 26.7 %collective-permute-done.rest_1_ = bf16[2560,256]{1,0:T(8,128)(2,1)S(1)} collective-permute-done((bf16[2560,256]{1,0:T(8,128)(2,1)}, bf16[2560,256]{1,0:T(8,128)(2,1)S(1)}, u32[]{:S(2)}, u32[]{:S(2)}) %collective-permute-start) | collective-permute-done | bytes 1310752 | tf_op jit(solution)/shard_map/ppermute | solution.py:462
  83.3 29.2 %collective-permute-done.1.rest_2_ = bf16[2560,256]{1,0:T(8,128)(2,1)S(1)} collective-permute-done((bf16[2560,256]{1,0:T(8,128)(2,1)}, bf16[2560,256]{1,0:T(8,128)(2,1)S(1)}, u32[]{:S(2)}, u32[]{:S(2)}) %collective-permute-start.1) | collective-permute-done | bytes 1310752 | tf_op jit(solution)/shard_map/ppermute | solution.py:462
  112.5 1.9 add_convert_fusion
  114.4 2.6 %collective-permute-start.3 = (bf16[1280,256]{1,0:T(8,128)(2,1)S(1)}, bf16[1280,256]{1,0:T(8,128)(2,1)S(1)}, u32[]{:S(2)}, u32[]{:S(2)}) collective-permute-start(bf16[1280,256]{1,0:T(8,128)(2,1)S(1)} %add_convert_fusion), channel_id=1, source_target_pairs={{0,1},{1,0},{2,3},{3,2},{4,5},{5,4},{6,7},{7,6},{8,9},{9,8},{10,11... | collective-permute-start | bytes 1966088 | tf_op jit(solution)/shard_map/ppermute | solution.py:468
  117.0 24.5 %collective-permute-done.3.rest_4_ = bf16[1280,256]{1,0:T(8,128)(2,1)S(1)} collective-permute-done((bf16[1280,256]{1,0:T(8,128)(2,1)S(1)}, bf16[1280,256]{1,0:T(8,128)(2,1)S(1)}, u32[]{:S(2)}, u32[]{:S(2)}) %collective-permute-start.3) | collective-permute-done | bytes 655392 | tf_op jit(solution)/shard_map/ppermute | solution.py:468
  141.5 0.9 copy-done.7
  142.4 10.3 %attend_own.1.state_ref = f32[2,8,256,256]{3,2,1,0:T(8,128)} custom-call(bf16[1,2,256,1024]{3,2,1,0:T(8,128)(2,1)} %q_ref.5, bf16[1,2,256,128]{3,2,1,0:T(8,128)(2,1)} %nk_ref.1, bf16[1,2,256,128]{3,2,1,0:T(8,128)(2,1)} %nv_ref.1, bf16[2560,256]{1,0:T(8,128)(2,1)} %get-tuple-element.20.rest_0_, bf16[2560,256]{1,0:T(8,128)(2,1)} %copy-done.3, ...), custom_call_target="tpu_custom_call" | custom-call | flops 2818572288 | bytes 9306112 | tf_op jit(solution)/shard_map/attend_own/pallas_call | solution.py:333
  152.6 27.3 %all-to-all-done.1.rest_0_.rest_1_.rest_2_.rest_3_.rest_4_.rest_5_.rest_6_.rest_7_ = bf16[32,400,256]{2,1,0:T(8,128)(2,1)} async-done(((bf16[32,400,256]{2,1,0:T(8,128)(2,1)}), bf16[32,400,256]{2,1,0:T(8,128)(2,1)}, u32[]{:S(2)}, u32[]{:S(2)}) %all-to-all-start.1) | async-done | bytes 6553632 | tf_op jit(solution)/shard_map/all_to_all | solution.py:460
  180.0 9.1 %all-to-all-start.2 = ((bf16[32,48,256]{2,1,0:T(8,128)(2,1)}), bf16[32,48,256]{2,1,0:T(8,128)(2,1)S(1)}, u32[]{:S(2)}, u32[]{:S(2)}) async-start(bf16[32,48,256]{2,1,0:T(8,128)(2,1)} %get-tuple-element.26), calls=%async_computation.2 | async-start | bytes 1572864 | tf_op jit(solution)/shard_map/all_to_all | solution.py:472
  189.1 0.5 and_select_fusion.place_ref
  189.6 21.9 %attend_main.1.state_ref = f32[2,8,256,256]{3,2,1,0:T(8,128)} custom-call(s32[16]{0:T(128)} %and_select_fusion.place_ref, bf16[1,2,256,1024]{3,2,1,0:T(8,128)(2,1)} %q_ref.5, f32[2,8,256,256]{3,2,1,0:T(8,128)} %attend_own.1.state_ref, bf16[32,400,256]{2,1,0:T(8,128)(2,1)} %all-to-all-done.1.rest_0_.rest_1_.rest_2_.rest_3_.rest_4_.rest_5_.rest_6_.rest_7_, ...), custom_call_target="tpu_custom_call" | custom-call | flops 10066329600 | bytes 11665408 | tf_op jit(solution)/shard_map/attend_main/pallas_call | solution.py:365
  211.6 0.0 all-to-all-done.2.arrived_ref
  211.6 2.2 copy-done
  213.8 6.0 %attend_last.1 = bf16[1,2,256,1024]{3,2,1,0:T(8,128)(2,1)} custom-call(s32[16]{0:T(128)S(1)} %copy-done.2, bf16[1,2,256,1024]{3,2,1,0:T(8,128)(2,1)S(1)} %copy-done.1, f32[2,8,256,256]{3,2,1,0:T(8,128)S(1)} %copy-done, bf16[32,48,256]{2,1,0:T(8,128)(2,1)S(1)} %all-to-all-done.2.arrived_ref), custom_call_target="tpu_custom_call" | custom-call | flops 1207959552 | bytes 8781824 | tf_op jit(solution)/shard_map/attend_last/pallas_call | solution.py:393
  (16 shorter events, 0.0 us)
Async XLA Ops:
  2.7 17.9 %all-to-all-start = ((s32[16,1,16]{2,1,0:T(1,128)}), s32[16,1,16]{2,1,0:T(1,128)S(1)}, u32[]{:S(2)}, u32[]{:S(2)}) async-start(s32[16,1,16]{2,1,0:T(1,128)} %broadcast_in_dim.26), calls=%async_computation | async-start | bytes 16384 | tf_op jit(solution)/shard_map/all_to_all | solution.py:437
  26.3 9.5 %copy-start.6 = (bf16[1,2,8,76,1024]{4,2,3,1,0:T(8,128)(2,1)S(1)}, bf16[1,2,8,76,1024]{4,2,3,1,0:T(8,128)(2,1)}, u32[]{:S(2)}) copy-start(bf16[1,2,8,76,1024]{4,2,3,1,0:T(8,128)(2,1)} %param.16) | copy-start | bytes 7471108
  26.3 153.7 %all-to-all-start.1 = ((bf16[32,400,256]{2,1,0:T(8,128)(2,1)}), bf16[32,400,256]{2,1,0:T(8,128)(2,1)}, u32[]{:S(2)}, u32[]{:S(2)}) async-start(bf16[32,400,256]{2,1,0:T(8,128)(2,1)} %get-tuple-element.18), calls=%async_computation.1 | async-start | bytes 13107200 | tf_op jit(solution)/shard_map/all_to_all | solution.py:460
  51.6 31.7 %collective-permute-start = (bf16[2560,256]{1,0:T(8,128)(2,1)}, bf16[2560,256]{1,0:T(8,128)(2,1)S(1)}, u32[]{:S(2)}, u32[]{:S(2)}) collective-permute-start(bf16[2560,256]{1,0:T(8,128)(2,1)} %get-tuple-element.21), channel_id=1, source_target_pairs={{0,2},{1,3},{2,4},{3,5},{4,6},{5,7},{6,0},{7,1},{8,10},{9,11},{10,... | collective-permute-start | bytes 3932168 | tf_op jit(solution)/shard_map/ppermute | solution.py:462
  52.9 59.6 %collective-permute-start.1 = (bf16[2560,256]{1,0:T(8,128)(2,1)}, bf16[2560,256]{1,0:T(8,128)(2,1)S(1)}, u32[]{:S(2)}, u32[]{:S(2)}) collective-permute-start(bf16[2560,256]{1,0:T(8,128)(2,1)} %get-tuple-element.22), channel_id=1, source_target_pairs={{0,4},{1,5},{2,6},{3,7},{4,0},{5,1},{6,2},{7,3},{8,12},{9,13},{10,... | collective-permute-start | bytes 3932168 | tf_op jit(solution)/shard_map/ppermute | solution.py:462
  55.5 57.0 %collective-permute-start.2 = (bf16[2560,256]{1,0:T(8,128)(2,1)}, bf16[2560,256]{1,0:T(8,128)(2,1)S(1)}, u32[]{:S(2)}, u32[]{:S(2)}) collective-permute-start(bf16[2560,256]{1,0:T(8,128)(2,1)} %get-tuple-element.23), channel_id=1, source_target_pairs={{0,6},{1,7},{2,0},{3,1},{4,2},{5,3},{6,4},{7,5},{8,14},{9,15},{10,... | collective-permute-start | bytes 3932168 | tf_op jit(solution)/shard_map/ppermute | solution.py:462
  83.3 31.1 %copy-start.3 = (bf16[2560,256]{1,0:T(8,128)(2,1)}, bf16[2560,256]{1,0:T(8,128)(2,1)S(1)}, u32[]{:S(2)}) copy-start(bf16[2560,256]{1,0:T(8,128)(2,1)S(1)} %collective-permute-done.rest_1_) | copy-start | bytes 3932164
  112.5 1.9 copy-start.4
  112.5 29.0 %copy-start.5 = (bf16[2560,256]{1,0:T(8,128)(2,1)}, bf16[2560,256]{1,0:T(8,128)(2,1)S(1)}, u32[]{:S(2)}) copy-start(bf16[2560,256]{1,0:T(8,128)(2,1)S(1)} %collective-permute-done.2.rest_3_) | copy-start | bytes 3932164
  114.4 27.1 %collective-permute-start.3 = (bf16[1280,256]{1,0:T(8,128)(2,1)S(1)}, bf16[1280,256]{1,0:T(8,128)(2,1)S(1)}, u32[]{:S(2)}, u32[]{:S(2)}) collective-permute-start(bf16[1280,256]{1,0:T(8,128)(2,1)S(1)} %add_convert_fusion), channel_id=1, source_target_pairs={{0,1},{1,0},{2,3},{3,2},{4,5},{5,4},{6,7},{7,6},{8,9},{9,8},{10,11... | collective-permute-start | bytes 1966088 | tf_op jit(solution)/shard_map/ppermute | solution.py:468
  141.5 0.9 copy-start.7
  180.0 31.6 %all-to-all-start.2 = ((bf16[32,48,256]{2,1,0:T(8,128)(2,1)}), bf16[32,48,256]{2,1,0:T(8,128)(2,1)S(1)}, u32[]{:S(2)}, u32[]{:S(2)}) async-start(bf16[32,48,256]{2,1,0:T(8,128)(2,1)} %get-tuple-element.26), calls=%async_computation.2 | async-start | bytes 1572864 | tf_op jit(solution)/shard_map/all_to_all | solution.py:472
  189.6 22.0 %copy-start.1 = (bf16[1,2,256,1024]{3,2,1,0:T(8,128)(2,1)S(1)}, bf16[1,2,256,1024]{3,2,1,0:T(8,128)(2,1)}, u32[]{:S(2)}) copy-start(bf16[1,2,256,1024]{3,2,1,0:T(8,128)(2,1)} %q_ref.5) | copy-start | bytes 3145732
  189.6 22.0 %copy-start.2 = (s32[16]{0:T(128)S(1)}, s32[16]{0:T(128)}, u32[]{:S(2)}) copy-start(s32[16]{0:T(128)} %and_select_fusion.place_ref) | copy-start | bytes 196
  211.6 2.2 copy-start

commit v6 on v5

--- a/solution.py
+++ b/solution.py
@@ -286,13 +286,32 @@
 
 
 def last_kernel(
-    place_ref, q_ref, state_ref, arrived_ref, out_ref, key_ref, wide_ref, done_ref, sem, *, kept
+    place_ref,
+    q_ref,
+    state_in,
+    arrived_ref,
+    out_ref,
+    state_ref,
+    key_ref,
+    wide_ref,
+    done_ref,
+    load_sem,
+    sem,
+    *,
+    kept,
 ):
     _, reqs, _, feats = q_ref.shape
     topk = place_ref.shape[0] // reqs
     rows = arrived_ref.shape[1]
     real = lax.broadcasted_iota(jnp.int32, (rows, HD), 0) < kept
     copies = []
+    loads = {}
+    for r in range(reqs):
+        for h in range(feats // HD):
+            loads[r, h] = pltpu.make_async_copy(
+                state_in.at[r, h], state_ref.at[r, h], load_sem.at[r, h]
+            )
+            loads[r, h].start()
     for r in range(reqs):
         for j in range(topk):
             span = slice(j * rows, (j + 1) * rows)
@@ -303,6 +322,7 @@
     for r in range(reqs):
         for h in range(feats // HD):
             lanes = slice(h * HD, (h + 1) * HD)
+            loads[r, h].wait()
             total, _ = attend_head(
                 q_ref[0, r, :, lanes], key_ref.at[r], wide_ref.at[r], state_ref[r, h], None
             )
@@ -392,16 +412,23 @@
     whole = pl.BlockSpec(memory_space=pltpu.VMEM)
     return pl.pallas_call(
         functools.partial(last_kernel, kept=kept),
-        in_specs=[pl.BlockSpec(memory_space=pltpu.SMEM), whole, whole, whole],
+        in_specs=[
+            pl.BlockSpec(memory_space=pltpu.SMEM),
+            whole,
+            pl.BlockSpec(memory_space=pl.ANY),
+            whole,
+        ],
         out_specs=pl.BlockSpec(memory_space=pl.ANY),
         out_shape=jax.ShapeDtypeStruct(queries.shape, jnp.bfloat16),
         scratch_shapes=[
+            pltpu.VMEM(state.shape, state.dtype),
             pltpu.VMEM((reqs, count, HD), jnp.bfloat16),
             pltpu.VMEM((reqs, count, 2 * HD), jnp.bfloat16),
             pltpu.VMEM((reqs, qlen, feats), jnp.bfloat16),
+            pltpu.SemaphoreType.DMA((reqs, heads)),
             pltpu.SemaphoreType.DMA((reqs,)),
         ],
-        compiler_params=pltpu.CompilerParams(vmem_limit_bytes=32 * MIB),
+        compiler_params=pltpu.CompilerParams(vmem_limit_bytes=48 * MIB),
         cost_estimate=attend_cost(reqs, heads, qlen, count),
         name="attend_last",
     )(place, queries, state, arrived)

time: 221 us -> 229 us (1.036)
  Pallas kernels: 62.5 us -> 69.7 us
    pallas_call x1, Pallas kernels: 5.96 us -> 14 us  [attend_last(): pl.pallas_call(functools.partial(last_kernel, kept=kept), in_specs=[pl.Bl...]
  transfers between devices with their start and end apart: 7 -> 7, of which waited for: 4 -> 4; matrix products, arithmetic and copies ran while one was open for 3% -> 3% of each run, Pallas kernels for 24% -> 23%
where the time goes in v6:
time: 229 us; the launch traced here: 228 us
  waiting for transfers between devices  108 us (47%)
  Pallas kernels  69.7 us (30%)
  starting transfers between devices  36.7 us (16%)
  local copies, waits for them, and re-layouts  8.55 us (4%)
  other arithmetic  5.24 us (2%)
    ppermute x3, waiting for transfers between devices, on_device(): lax.ppermute(piece, 'tensor', [(i, moved(i, (shift, 0))) for i in range(p...  55.9 us
    all_to_all x1, waiting for transfers between devices, on_device(): arrived = lax.all_to_all(main, ('section', 'dp'), 0, 0, tiled=True)  27.4 us
    ppermute x1, waiting for transfers between devices, on_device(): lax.ppermute(across, 'tensor', [(i, moved(i, (0, 1))) for i in range(part...  24.6 us
    pallas_call x1, Pallas kernels, attend_main(): pl.pallas_call(main_kernel, grid_spec=pltpu.PrefetchScalarGridSpec(num_sc...  21.9 us
    pallas_call x1, Pallas kernels, attend_last(): pl.pallas_call(functools.partial(last_kernel, kept=kept), in_specs=[pl.Bl...  14 us
    pallas_call x1, Pallas kernels, project(): pl.pallas_call(functools.partial(project_kernel, rrows=rrows, slot=slot),...  13 us
    pallas_call x1, Pallas kernels, attend_own(): pl.pallas_call(functools.partial(own_kernel, rrows=rrows, slot=slot), gri...  10.3 us
    all_to_all x1, starting transfers between devices, on_device(): arrived = lax.all_to_all(main, ('section', 'dp'), 0, 0, tiled=True)  10.1 us
  transfers between devices with their start and end apart: 7, of which 4 were waited for; matrix products, arithmetic and copies ran while one was open for 3% of the time, Pallas kernels for 23%

profile of v6, /device:TPU:1, one launch (start us, length us, event | category | flops | bytes accessed | tf_op | source)
XLA Modules:
  0.0 228.4 jit_solution(2497057105909852608)
XLA Ops:
  0.0 0.7 compare_select_fusion
  0.7 0.1 reshape.19
  0.8 1.3 gather_fusion
  2.1 0.6 broadcast_in_dim.26
  2.7 10.0 %all-to-all-start = ((s32[16,1,16]{2,1,0:T(1,128)}), s32[16,1,16]{2,1,0:T(1,128)S(1)}, u32[]{:S(2)}, u32[]{:S(2)}) async-start(s32[16,1,16]{2,1,0:T(1,128)} %broadcast_in_dim.26), calls=%async_computation | async-start | bytes 16384 | tf_op jit(solution)/shard_map/all_to_all | solution.py:464
  12.7 1.4 select_reduce_fusion.ids_ref
  14.2 6.5 %compact.1.packed_ref = bf16[2,8,448,256]{3,2,1,0:T(8,128)(2,1)} custom-call(s32[8]{0:T(128)} %select_reduce_fusion.ids_ref, s32[76,256]{1,0:T(8,128)} %bitcast.10, bf16[2,8,512,128]{3,2,1,0:T(8,128)(2,1)} %ck_ref.1, bf16[2,8,512,128]{3,2,1,0:T(8,128)(2,1)} %cv_ref.1), custom_call_target="tpu_custom_call" | custom-call | flops 1879048192 | bytes 8388608 | tf_op jit(solution)/shard_map/compact/pallas_call | solution.py:59
  20.7 0.7 fusion.2.local_ref
  21.4 4.0 %spread.1 = (bf16[32,400,256]{2,1,0:T(8,128)(2,1)}, bf16[32,48,256]{2,1,0:T(8,128)(2,1)}) custom-call(s32[16]{0:T(128)} %fusion.2.local_ref, bf16[2,8,448,256]{3,2,1,0:T(8,128)(2,1)} %compact.1.packed_ref), custom_call_target="tpu_custom_call" | custom-call | bytes 11010048 | tf_op jit(solution)/shard_map/spread/pallas_call | solution.py:126
  25.4 0.0 copy-start.6
  25.4 10.1 %all-to-all-start.1 = ((bf16[32,400,256]{2,1,0:T(8,128)(2,1)}), bf16[32,400,256]{2,1,0:T(8,128)(2,1)}, u32[]{:S(2)}, u32[]{:S(2)}) async-start(bf16[32,400,256]{2,1,0:T(8,128)(2,1)} %get-tuple-element.18), calls=%async_computation.1 | async-start | bytes 13107200 | tf_op jit(solution)/shard_map/all_to_all | solution.py:487
  35.5 0.6 stack.35.dest_ref
  36.2 2.8 %copy.15.hidden_ref = bf16[1,2,8,76,1024]{4,3,2,1,0:T(8,128)(2,1)} copy(bf16[1,2,8,76,1024]{4,2,3,1,0:T(8,128)(2,1)S(1)} %copy-done.6) | data formatting | bytes 4980736 | tf_op jit(solution)/shard_map/optimization_barrier | solution.py:478
  39.0 13.0 %project.1 = (bf16[2560,256]{1,0:T(8,128)(2,1)}, bf16[2560,256]{1,0:T(8,128)(2,1)}, bf16[2560,256]{1,0:T(8,128)(2,1)}, bf16[2560,256]{1,0:T(8,128)(2,1)}) custom-call(s32[8]{0:T(128)} %stack.35.dest_ref, bf16[1,2,8,76,1024]{4,3,2,1,0:T(8,128)(2,1)} %copy.15.hidden_ref, bf16[1,1024,1024]{2,1,0:T(8,128)(2,1)} %wk_ref.1, bf16[1,1024,1024]{2,1,0:T(8,128)(2,1)} %wv_ref.1), custom_call_target="tpu_custom_call" | custom-call | flops 5368709120 | bytes 11927552 | tf_op jit(solution)/shard_map/project/pallas_call | solution.py:180
  52.0 1.3 collective-permute-start
  53.3 2.6 %collective-permute-start.1 = (bf16[2560,256]{1,0:T(8,128)(2,1)}, bf16[2560,256]{1,0:T(8,128)(2,1)S(1)}, u32[]{:S(2)}, u32[]{:S(2)}) collective-permute-start(bf16[2560,256]{1,0:T(8,128)(2,1)} %get-tuple-element.22), channel_id=1, source_target_pairs={{0,4},{1,5},{2,6},{3,7},{4,0},{5,1},{6,2},{7,3},{8,12},{9,13},{10,... | collective-permute-start | bytes 3932168 | tf_op jit(solution)/shard_map/ppermute | solution.py:489
  55.9 1.1 collective-permute-start.2
  57.0 26.7 %collective-permute-done.rest_1_ = bf16[2560,256]{1,0:T(8,128)(2,1)S(1)} collective-permute-done((bf16[2560,256]{1,0:T(8,128)(2,1)}, bf16[2560,256]{1,0:T(8,128)(2,1)S(1)}, u32[]{:S(2)}, u32[]{:S(2)}) %collective-permute-start) | collective-permute-done | bytes 1310752 | tf_op jit(solution)/shard_map/ppermute | solution.py:489
  83.7 29.2 %collective-permute-done.1.rest_2_ = bf16[2560,256]{1,0:T(8,128)(2,1)S(1)} collective-permute-done((bf16[2560,256]{1,0:T(8,128)(2,1)}, bf16[2560,256]{1,0:T(8,128)(2,1)S(1)}, u32[]{:S(2)}, u32[]{:S(2)}) %collective-permute-start.1) | collective-permute-done | bytes 1310752 | tf_op jit(solution)/shard_map/ppermute | solution.py:489
  112.9 0.0 collective-permute-done.2.rest_3_
  112.9 1.9 add_convert_fusion
  114.8 2.5 %collective-permute-start.3 = (bf16[1280,256]{1,0:T(8,128)(2,1)S(1)}, bf16[1280,256]{1,0:T(8,128)(2,1)S(1)}, u32[]{:S(2)}, u32[]{:S(2)}) collective-permute-start(bf16[1280,256]{1,0:T(8,128)(2,1)S(1)} %add_convert_fusion), channel_id=1, source_target_pairs={{0,1},{1,0},{2,3},{3,2},{4,5},{5,4},{6,7},{7,6},{8,9},{9,8},{10,11... | collective-permute-start | bytes 1966088 | tf_op jit(solution)/shard_map/ppermute | solution.py:495
  117.4 24.6 %collective-permute-done.3.rest_4_ = bf16[1280,256]{1,0:T(8,128)(2,1)S(1)} collective-permute-done((bf16[1280,256]{1,0:T(8,128)(2,1)S(1)}, bf16[1280,256]{1,0:T(8,128)(2,1)S(1)}, u32[]{:S(2)}, u32[]{:S(2)}) %collective-permute-start.3) | collective-permute-done | bytes 655392 | tf_op jit(solution)/shard_map/ppermute | solution.py:495
  141.9 0.9 copy-done.7
  142.8 10.3 %attend_own.1.state_ref = f32[2,8,256,256]{3,2,1,0:T(8,128)} custom-call(bf16[1,2,256,1024]{3,2,1,0:T(8,128)(2,1)} %q_ref.5, bf16[1,2,256,128]{3,2,1,0:T(8,128)(2,1)} %nk_ref.1, bf16[1,2,256,128]{3,2,1,0:T(8,128)(2,1)} %nv_ref.1, bf16[2560,256]{1,0:T(8,128)(2,1)} %get-tuple-element.20.rest_0_, bf16[2560,256]{1,0:T(8,128)(2,1)} %copy-done.3, ...), custom_call_target="tpu_custom_call" | custom-call | flops 2818572288 | bytes 9306112 | tf_op jit(solution)/shard_map/attend_own/pallas_call | solution.py:353
  153.0 27.4 %all-to-all-done.1.rest_0_.rest_1_.rest_2_.rest_3_.rest_4_.rest_5_.rest_6_.rest_7_ = bf16[32,400,256]{2,1,0:T(8,128)(2,1)} async-done(((bf16[32,400,256]{2,1,0:T(8,128)(2,1)}), bf16[32,400,256]{2,1,0:T(8,128)(2,1)}, u32[]{:S(2)}, u32[]{:S(2)}) %all-to-all-start.1) | async-done | bytes 6553632 | tf_op jit(solution)/shard_map/all_to_all | solution.py:487
  180.4 9.1 %all-to-all-start.2 = ((bf16[32,48,256]{2,1,0:T(8,128)(2,1)}), bf16[32,48,256]{2,1,0:T(8,128)(2,1)S(1)}, u32[]{:S(2)}, u32[]{:S(2)}) async-start(bf16[32,48,256]{2,1,0:T(8,128)(2,1)} %get-tuple-element.26), calls=%async_computation.2 | async-start | bytes 1572864 | tf_op jit(solution)/shard_map/all_to_all | solution.py:499
  189.5 0.5 and_select_fusion.place_ref
  190.0 21.9 %attend_main.1.state_in = f32[2,8,256,256]{3,2,1,0:T(8,128)} custom-call(s32[16]{0:T(128)} %and_select_fusion.place_ref, bf16[1,2,256,1024]{3,2,1,0:T(8,128)(2,1)} %q_ref.5, f32[2,8,256,256]{3,2,1,0:T(8,128)} %attend_own.1.state_ref, bf16[32,400,256]{2,1,0:T(8,128)(2,1)} %all-to-all-done.1.rest_0_.rest_1_.rest_2_.rest_3_.rest_4_.rest_5_.rest_6_.rest_7_, ...), custom_call_target="tpu_custom_call" | custom-call | flops 10066329600 | bytes 11665408 | tf_op jit(solution)/shard_map/attend_main/pallas_call | solution.py:385
  211.9 0.0 all-to-all-done.2.arrived_ref
  212.0 2.2 copy-done
  214.2 14.0 %attend_last.1 = bf16[1,2,256,1024]{3,2,1,0:T(8,128)(2,1)} custom-call(s32[16]{0:T(128)S(1)} %copy-done.2, bf16[1,2,256,1024]{3,2,1,0:T(8,128)(2,1)S(1)} %copy-done.1, f32[2,8,256,256]{3,2,1,0:T(8,128)S(1)} %copy-done, bf16[32,48,256]{2,1,0:T(8,128)(2,1)S(1)} %all-to-all-done.2.arrived_ref), custom_call_target="tpu_custom_call" | custom-call | flops 1207959552 | bytes 8781824 | tf_op jit(solution)/shard_map/attend_last/pallas_call | solution.py:413
  (16 shorter events, 0.0 us)
Async XLA Ops:
  2.7 17.9 %all-to-all-start = ((s32[16,1,16]{2,1,0:T(1,128)}), s32[16,1,16]{2,1,0:T(1,128)S(1)}, u32[]{:S(2)}, u32[]{:S(2)}) async-start(s32[16,1,16]{2,1,0:T(1,128)} %broadcast_in_dim.26), calls=%async_computation | async-start | bytes 16384 | tf_op jit(solution)/shard_map/all_to_all | solution.py:464
  25.4 10.8 %copy-start.6 = (bf16[1,2,8,76,1024]{4,2,3,1,0:T(8,128)(2,1)S(1)}, bf16[1,2,8,76,1024]{4,2,3,1,0:T(8,128)(2,1)}, u32[]{:S(2)}) copy-start(bf16[1,2,8,76,1024]{4,2,3,1,0:T(8,128)(2,1)} %param.16) | copy-start | bytes 7471108
  25.4 155.0 %all-to-all-start.1 = ((bf16[32,400,256]{2,1,0:T(8,128)(2,1)}), bf16[32,400,256]{2,1,0:T(8,128)(2,1)}, u32[]{:S(2)}, u32[]{:S(2)}) async-start(bf16[32,400,256]{2,1,0:T(8,128)(2,1)} %get-tuple-element.18), calls=%async_computation.1 | async-start | bytes 13107200 | tf_op jit(solution)/shard_map/all_to_all | solution.py:487
  52.0 31.7 %collective-permute-start = (bf16[2560,256]{1,0:T(8,128)(2,1)}, bf16[2560,256]{1,0:T(8,128)(2,1)S(1)}, u32[]{:S(2)}, u32[]{:S(2)}) collective-permute-start(bf16[2560,256]{1,0:T(8,128)(2,1)} %get-tuple-element.21), channel_id=1, source_target_pairs={{0,2},{1,3},{2,4},{3,5},{4,6},{5,7},{6,0},{7,1},{8,10},{9,11},{10,... | collective-permute-start | bytes 3932168 | tf_op jit(solution)/shard_map/ppermute | solution.py:489
  53.3 59.6 %collective-permute-start.1 = (bf16[2560,256]{1,0:T(8,128)(2,1)}, bf16[2560,256]{1,0:T(8,128)(2,1)S(1)}, u32[]{:S(2)}, u32[]{:S(2)}) collective-permute-start(bf16[2560,256]{1,0:T(8,128)(2,1)} %get-tuple-element.22), channel_id=1, source_target_pairs={{0,4},{1,5},{2,6},{3,7},{4,0},{5,1},{6,2},{7,3},{8,12},{9,13},{10,... | collective-permute-start | bytes 3932168 | tf_op jit(solution)/shard_map/ppermute | solution.py:489
  55.9 57.0 %collective-permute-start.2 = (bf16[2560,256]{1,0:T(8,128)(2,1)}, bf16[2560,256]{1,0:T(8,128)(2,1)S(1)}, u32[]{:S(2)}, u32[]{:S(2)}) collective-permute-start(bf16[2560,256]{1,0:T(8,128)(2,1)} %get-tuple-element.23), channel_id=1, source_target_pairs={{0,6},{1,7},{2,0},{3,1},{4,2},{5,3},{6,4},{7,5},{8,14},{9,15},{10,... | collective-permute-start | bytes 3932168 | tf_op jit(solution)/shard_map/ppermute | solution.py:489
  83.7 31.1 %copy-start.3 = (bf16[2560,256]{1,0:T(8,128)(2,1)}, bf16[2560,256]{1,0:T(8,128)(2,1)S(1)}, u32[]{:S(2)}) copy-start(bf16[2560,256]{1,0:T(8,128)(2,1)S(1)} %collective-permute-done.rest_1_) | copy-start | bytes 3932164
  112.9 1.9 copy-start.4
  112.9 29.0 %copy-start.5 = (bf16[2560,256]{1,0:T(8,128)(2,1)}, bf16[2560,256]{1,0:T(8,128)(2,1)S(1)}, u32[]{:S(2)}) copy-start(bf16[2560,256]{1,0:T(8,128)(2,1)S(1)} %collective-permute-done.2.rest_3_) | copy-start | bytes 3932164
  114.8 27.1 %collective-permute-start.3 = (bf16[1280,256]{1,0:T(8,128)(2,1)S(1)}, bf16[1280,256]{1,0:T(8,128)(2,1)S(1)}, u32[]{:S(2)}, u32[]{:S(2)}) collective-permute-start(bf16[1280,256]{1,0:T(8,128)(2,1)S(1)} %add_convert_fusion), channel_id=1, source_target_pairs={{0,1},{1,0},{2,3},{3,2},{4,5},{5,4},{6,7},{7,6},{8,9},{9,8},{10,11... | collective-permute-start | bytes 1966088 | tf_op jit(solution)/shard_map/ppermute | solution.py:495
  141.9 0.9 copy-start.7
  180.4 31.6 %all-to-all-start.2 = ((bf16[32,48,256]{2,1,0:T(8,128)(2,1)}), bf16[32,48,256]{2,1,0:T(8,128)(2,1)S(1)}, u32[]{:S(2)}, u32[]{:S(2)}) async-start(bf16[32,48,256]{2,1,0:T(8,128)(2,1)} %get-tuple-element.26), calls=%async_computation.2 | async-start | bytes 1572864 | tf_op jit(solution)/shard_map/all_to_all | solution.py:499
  190.0 21.9 %copy-start.1 = (bf16[1,2,256,1024]{3,2,1,0:T(8,128)(2,1)S(1)}, bf16[1,2,256,1024]{3,2,1,0:T(8,128)(2,1)}, u32[]{:S(2)}) copy-start(bf16[1,2,256,1024]{3,2,1,0:T(8,128)(2,1)} %q_ref.5) | copy-start | bytes 3145732
  190.0 21.9 %copy-start.2 = (s32[16]{0:T(128)S(1)}, s32[16]{0:T(128)}, u32[]{:S(2)}) copy-start(s32[16]{0:T(128)} %and_select_fusion.place_ref) | copy-start | bytes 196
  212.0 2.2 copy-start
